TPU v7x, 32 devices: a whole 2x2x4 slice. The times are simulated.
32 devices in a mesh: groups: 2 (over x), latent: 16 (over z, y, core).
Axes of the slice: x: 2, y: 2, z: 4, core: 2. Of those that a mesh axis runs over, the one named last changes fastest.
Arguments:
- row_store: bfloat16 [1024, 2, 4608], P(('groups', 'latent')), parts along dimension 0, may hold values from -6 to 6
- row_slot: int32 [512], P('groups'), parts along dimension 0, may hold values from 0 to 511, as said below
- targets: bfloat16 [512, 2, 4608], P(('groups', 'latent')), parts along dimension 0, may hold values from -6 to 6
- enc_weight: bfloat16 [4, 4608, 2048], P('groups', None, 'latent'), parts along dimension 0, may hold values from -0.09375 to 0.09375
- enc_bias: float32 [4, 2048], P('groups', 'latent'), parts along dimension 0, may hold values from -1 to 1
- dec_weight: bfloat16 [6, 2048, 4608], P('groups', 'latent'), parts along dimension 0, may hold values from -0.125 to 0.125
- dec_bias: float32 [4, 4608], P('groups'), parts along dimension 0, may hold values from -5 to 5
Outputs:
- rebuilt: float32 [512, 2, 4608], P(('groups', 'latent')), parts along dimension 0
- grad_enc: bfloat16 [4, 4608, 2048], P('groups', None, 'latent'), parts along dimension 0
- grad_ebias: float32 [4, 2048], P('groups', 'latent'), parts along dimension 0
- grad_dec: bfloat16 [6, 2048, 4608], P('groups', 'latent'), parts along dimension 0
- grad_dbias: float32 [4, 4608], P('groups'), parts along dimension 0
There are 2 independent parts, one for each index of `groups`. A program takes and returns all parts, laid end to end along the dimension named above; each array names one. Nothing has to cross between parts.
Inputs may be any that keep to these rules, and one draw needn't show every extreme that they name: The slots row_slot holds are distinct. Slot k belongs to owner k // 32; an owner's slots of this batch are its first ones in a row, with no gap. Owners hold 0 to 32 rows of the batch, and in every draw some owner holds exactly 32.
All inputs are finite; a program needn't handle non-finite values.
Results may differ from a plain program's by a relative error of at most 0.0058.
Values may be sent and summed in bfloat16 or wider, within the bound.
A program may use at most 128 MiB of HBM per device.

v0:
```python
import math

import jax
import jax.numpy as jnp
from jax import lax
from jax.sharding import PartitionSpec as P


def pair_index(source, target, layers):
    return source * layers - source * (source - 1) // 2 + target - source


def activate(values):
    return jax.nn.gelu(values, approximate=True)


def recon_terms(target, latents, dec_weight, layers):
    summed_terms = None
    for source in range(target + 1):
        block = latents[source]
        product = jnp.dot(
            block,
            dec_weight[pair_index(source, target, layers)],
            preferred_element_type=jnp.float32,
        )
        summed_terms = product if summed_terms is None else summed_terms + product
    return summed_terms


def body(row_store, row_slot, targets, enc_weight, enc_bias, dec_weight, dec_bias):
    layers = enc_weight.shape[0]
    row_count = row_slot.shape[0]
    gathered = lax.all_gather(row_store, "latent", axis=0, tiled=True)
    inputs = jnp.take(gathered, row_slot, axis=0)
    pre_list = []
    latents = []
    for source in range(layers):
        pre_acts = (
            jnp.dot(inputs[:, source], enc_weight[source], preferred_element_type=jnp.float32)
            + enc_bias[source][None, :]
        )
        pre_list.append(pre_acts)
        latents.append(activate(pre_acts).astype(jnp.bfloat16))
    stacked = jnp.stack(
        [recon_terms(target, latents, dec_weight, layers) for target in range(layers)], axis=1
    )
    summed = lax.psum_scatter(stacked, "latent", scatter_dimension=0, tiled=True)
    rebuilt = summed + dec_bias[None, :, :]
    factor = 1.0 / math.sqrt(row_count)
    error_part = ((rebuilt - targets.astype(jnp.float32)) * factor).astype(jnp.bfloat16)
    errors = lax.all_gather(error_part, "latent", axis=0, tiled=True)
    grad_dec_list = []
    for source in range(layers):
        for target in range(source, layers):
            grad_dec_list.append(
                jnp.dot(
                    latents[source].T, errors[:, target], preferred_element_type=jnp.float32
                ).astype(jnp.bfloat16)
            )
    grad_dec = jnp.stack(grad_dec_list, axis=0)
    grad_dbias = jnp.sum(errors.astype(jnp.float32), axis=0)
    grad_enc_list = []
    grad_ebias_list = []
    for source in range(layers):
        back = None
        for target in range(source, layers):
            product = lax.dot_general(
                errors[:, target],
                dec_weight[pair_index(source, target, layers)],
                (((1,), (1,)), ((), ())),
                preferred_element_type=jnp.float32,
            )
            back = product if back is None else back + product
        unused, pullback = jax.vjp(activate, pre_list[source])
        dpre = pullback(back)[0]
        grad_ebias_list.append(jnp.sum(dpre, axis=0))
        grad_enc_list.append(
            jnp.dot(
                inputs[:, source].T, dpre.astype(jnp.bfloat16), preferred_element_type=jnp.float32
            ).astype(jnp.bfloat16)
        )
    grad_enc = jnp.stack(grad_enc_list, axis=0)
    grad_ebias = jnp.stack(grad_ebias_list, axis=0)
    return (rebuilt, grad_enc, grad_ebias, grad_dec, grad_dbias)


def solution(mesh):
    in_specs = (
        P(("groups", "latent"), None, None),
        P("groups"),
        P(("groups", "latent"), None, None),
        P("groups", None, "latent"),
        P("groups", "latent"),
        P("groups", "latent", None),
        P("groups", None),
    )
    out_specs = (
        P(("groups", "latent"), None, None),
        P("groups", None, "latent"),
        P("groups", "latent"),
        P("groups", "latent", None),
        P("groups", None),
    )
    return jax.shard_map(body, mesh=mesh, in_specs=in_specs, out_specs=out_specs, check_vma=False)
```

profile of v0, /device:TPU:0, one launch (start us, length us, event | category | flops | bytes accessed | tf_op | source)
XLA Modules:
  0.0 332.6 jit_solution(13572316347058667284)
XLA Ops:
  7.2 0.7 all-gather.3.cloned.1.call-update
  7.9 0.7 compare_select_fusion
  8.6 0.7 compare_and_fusion
  9.3 0.8 slice_bitcast_fusion.14
  10.1 84.4 %all-gather.3.cloned.1.call-done = bf16[512,2,4608]{2,1,0:T(2,128)(2,1)} async-done(((bf16[32,2,4608]{2,1,0:T(2,128)(2,1)}), bf16[512,2,4608]{2,1,0:T(2,128)(2,1)}) %all-gather.3.cloned.1.call-update) | async-done | bytes 9437200 | tf_op jit(solution)/shard_map/all_gather | solution.py:33
  94.5 19.2 %gather_fusion = bf16[256,2,4608]{2,1,0:T(2,128)(2,1)} fusion(bf16[512,2,4608]{2,1,0:T(2,128)(2,1)} %all-gather.3.cloned.1.call-done, s32[1024]{0:T(1024)S(1)} %pad_clamp_fusion), kind=kCustom, calls=%fused_computation | custom fusion | bytes 9438208 | tf_op jit(solution)/shard_map/jit(_take)/gather | solution.py:34
  113.6 9.0 %broadcast_select_fusion = bf16[256,2,4608]{2,1,0:T(2,128)(2,1)} fusion(bf16[256,2,4608]{2,1,0:T(2,128)(2,1)} %gather_fusion, pred[256]{0:T(512)(128)(4,1)S(1)} %compare_and_fusion), kind=kLoop, calls=%fused_computation.3 | loop fusion | flops 2359296 | bytes 9437440 | tf_op jit(solution)/shard_map/jit(_take)/select_n | solution.py:34
  122.7 9.8 %fusion.67 = (bf16[256,1,4608]{2,1,0:T(2,128)(2,1)S(1)}, bf16[256,1,4608]{2,1,0:T(2,128)(2,1)S(1)}) fusion(bf16[256,2,4608]{2,1,0:T(2,128)(2,1)} %broadcast_select_fusion), kind=kLoop, calls=%fused_computation.82 | loop fusion | bytes 9437184 | tf_op jit(solution)/shard_map/slice | solution.py:39
  132.5 1.4 multiply_convert_fusion.2
  133.9 1.0 copy-done.1
  135.0 2.2 copy-done.3
  137.1 0.8 fusion.19
  137.9 0.8 convolution_bitcast_fusion
  138.7 0.8 fusion.34
  139.4 0.8 fusion
  140.2 4.3 %pad_maximum_fusion = f32[256,2,4608]{2,0,1:T(8,128)} fusion(f32[256,1,4608]{2,0,1:T(8,128)S(1)} %fusion, f32[256,1,4608]{2,0,1:T(8,128)S(1)} %convolution_bitcast_fusion), kind=kLoop, calls=%fused_computation.1 | loop fusion | flops 2359296 | bytes 18874368 | tf_op jit(solution)/shard_map/stack | solution.py:44
  144.5 109.6 %reduce-scatter.2.cloned.1.call-done = f32[16,2,4608]{2,0,1:T(8,128)} async-done(((f32[256,2,4608]{2,0,1:T(8,128)}), f32[16,2,4608]{2,0,1:T(8,128)}) %reduce-scatter.2.cloned.1.call-update) | async-done | bytes 589840 | tf_op jit(solution)/shard_map/reduce_scatter | solution.py:47
  254.1 2.1 multiply_convert_fusion
  256.3 2.3 copy.19
  258.6 51.8 %all-gather.5.cloned.1.call-done = bf16[256,2,4608]{2,0,1:T(8,128)(2,1)} async-done(((bf16[16,2,4608]{2,0,1:T(8,128)(2,1)}), bf16[256,2,4608]{2,0,1:T(8,128)(2,1)}) %all-gather.5.cloned.1.call-update) | async-done | bytes 4718608 | tf_op jit(solution)/shard_map/all_gather | solution.py:51
  310.4 2.6 fusion.68
  313.1 3.3 fusion.2
  316.4 0.8 fusion.12
  317.2 0.8 fusion.69
  318.0 0.8 fusion.1
  318.9 0.6 pad_maximum_fusion.3
  319.5 1.6 pad_maximum_fusion.2
  321.1 0.5 fusion.5
  321.6 0.5 fusion.4
  322.1 0.5 fusion.3
  322.6 2.0 pad_maximum_fusion.1
  324.6 1.4 convert_reduce_fusion
  (29 shorter events, 0.2 us)
Async XLA Ops:
  7.2 87.3 %all-gather.3.cloned.1.call-start = ((), (), s32[]{:S(2)}) async-start(), calls=%async_computation.1 | async-start | bytes 10027008 | tf_op jit(solution)/shard_map/all_gather | solution.py:33
  7.9 246.2 %reduce-scatter.2.cloned.1.call-start = ((), (), s32[]{:S(2)}) async-start(), calls=%async_computation.2 | async-start | bytes 10027008 | tf_op jit(solution)/shard_map/reduce_scatter | solution.py:47
  122.7 9.9 %copy-start.8 = (bf16[2,4608,128]{2,1,0:T(8,128)(2,1)S(1)}, bf16[2,4608,128]{2,1,0:T(8,128)(2,1)}, u32[]{:S(2)}) copy-start(bf16[2,4608,128]{2,1,0:T(8,128)(2,1)} %param.10) | copy-start | bytes 7077892
  132.5 2.5 copy-start.1
  132.5 6.1 %copy-start.2 = (bf16[256,1,4608]{2,1,0:T(2,128)(2,1)}, bf16[256,1,4608]{2,1,0:T(2,128)(2,1)S(1)}, u32[]{:S(2)}) copy-start(bf16[256,1,4608]{2,1,0:T(2,128)(2,1)S(1)} %get-tuple-element.27) | copy-start | bytes 7077892
  132.5 4.6 %copy-start.3 = (bf16[3,128,4608]{2,1,0:T(8,128)(2,1)S(1)}, bf16[3,128,4608]{2,1,0:T(8,128)(2,1)}, u32[]{:S(2)}) copy-start(bf16[3,128,4608]{2,1,0:T(8,128)(2,1)} %param.12) | copy-start | bytes 10616836
  134.9 3.7 %copy-start.4 = (bf16[256,128]{1,0:T(8,128)(2,1)}, bf16[256,128]{1,0:T(8,128)(2,1)S(1)}, u32[]{:S(2)}) copy-start(bf16[256,128]{1,0:T(8,128)(2,1)S(1)} %get-tuple-element.31) | copy-start | bytes 196612
  139.4 0.8 copy-start.6
  144.5 166.0 %all-gather.5.cloned.1.call-start = ((), (), s32[]{:S(2)}) async-start(), calls=%async_computation.3 | async-start | bytes 5013504 | tf_op jit(solution)/shard_map/all_gather | solution.py:51
  310.4 5.9 %copy-start = (bf16[256,2,4608]{2,0,1:T(8,128)(2,1)S(1)}, bf16[256,2,4608]{2,0,1:T(8,128)(2,1)}, u32[]{:S(2)}) copy-start(bf16[256,2,4608]{2,0,1:T(8,128)(2,1)} %all-gather.5.cloned.1.call-done) | copy-start | bytes 14155780
  313.1 4.1 %copy-start.9 = (f32[256,128]{1,0:T(8,128)S(1)}, f32[256,128]{1,0:T(8,128)}, u32[]{:S(2)}) copy-start(f32[256,128]{1,0:T(8,128)} %get-tuple-element.32) | copy-start | bytes 393220
  313.1 4.9 %slice-start = ((s8[4718592]{0:T(1024)(128)(4,1)}), s8[4194304]{0:T(1024)(128)(4,1)S(1)}, s32[]{:S(2)}) async-start(s8[4718592]{0:T(1024)(128)(4,1)} %bitcast.99), calls=%async_computation.4 | async-start | bytes 8388608
  316.4 1.6 slice-start.1
  318.0 3.0 copy-start.7
  319.5 2.2 copy-start.5
Sparse Core Ops, SparseCore 0:
  10.3 84.1 all-gather.2
  144.6 109.4 reduce-scatter.1
  257.3 53.1 all-gather.4
where the time goes:
time: 333 us
  waiting for transfers between devices  246 us (74%)
  local copies, waits for them, and re-layouts  35.3 us (11%)
  other arithmetic  22.4 us (7%)
  matrix products  14.3 us (4%)
  between operations  14 us (4%)
    reduce_scatter x1, waiting for transfers between devices, body(): lax.psum_scatter(stacked, 'latent', scatter_dimension=0, tiled=True)  110 us
    all_gather x1, waiting for transfers between devices, body(): gathered = lax.all_gather(row_store, 'latent', axis=0, tiled=True)  84.4 us
    all_gather x1, waiting for transfers between devices, body(): errors = lax.all_gather(error_part, 'latent', axis=0, tiled=True)  51.8 us
    gather x1, local copies, waits for them, and re-layouts, body(): inputs = jnp.take(gathered, row_slot, axis=0)  19.2 us
    slice x1, local copies, waits for them, and re-layouts, body(): inputs[:, source]  9.82 us
    select_n x2, other arithmetic, body(): inputs = jnp.take(gathered, row_slot, axis=0)  9.7 us
  transfers between devices with their start and end apart: 3, of which 3 were waited for; matrix products, arithmetic and copies ran while one was open for 1% of the time, Pallas kernels for 0%

commit v1 on v0

v1 whole, which is shorter than its diff:
```python
import functools
import math

import jax
import jax.numpy as jnp
from jax import lax
from jax.experimental import pallas as pl
from jax.experimental.pallas import tpu as pltpu
from jax.sharding import PartitionSpec as P

MESH = pl.DeviceIdType.MESH
VMEM_LIMIT = 56 * 1024 * 1024


def pair_index(source, target, layers):
    return source * layers - source * (source - 1) // 2 + target - source


def activate(values):
    return jax.nn.gelu(values, approximate=True)


def recon_terms(target, latents, dec_weight, layers):
    summed_terms = None
    for source in range(target + 1):
        product = jnp.dot(
            latents[source],
            dec_weight[pair_index(source, target, layers)],
            preferred_element_type=jnp.float32,
        )
        summed_terms = product if summed_terms is None else summed_terms + product
    return summed_terms


def position():
    me = lax.axis_index("latent")
    return me // 4, (me // 2) % 2, me % 2


def greet(long, z, y, c):
    barrier = pltpu.get_barrier_semaphore()

    def signal(zz, yy, cc):
        pl.semaphore_signal(
            barrier, inc=1, device_id={"latent": zz * 4 + yy * 2 + cc}, device_id_type=MESH
        )

    signal(z, y, 1 - c)
    signal(z, 1 - y, c)

    @pl.when(z > 0)
    def _():
        signal(z - 1, y, c)

    @pl.when(z < long - 1)
    def _():
        signal(z + 1, y, c)

    peers = 2 + (z > 0).astype(jnp.int32) + (z < long - 1).astype(jnp.int32)
    pl.semaphore_wait(barrier, peers)


def gather_steps(long, rows, z, y, c, whole, first_ref, send_sem, recv_sem):
    def index(zz, yy, cc):
        return zz * 4 + yy * 2 + cc

    def block(owner):
        return whole.at[:, pl.ds(pl.multiple_of(owner * rows, rows), rows), :]

    def copy(kind, owner, target, src=None):
        return pltpu.make_async_remote_copy(
            src_ref=block(owner) if src is None else src,
            dst_ref=block(owner),
            send_sem=send_sem.at[kind, owner],
            recv_sem=recv_sem.at[owner],
            device_id={"latent": target},
            device_id_type=MESH,
        )

    me = index(z, y, c)
    left, right = index(z - 1, y, c), index(z + 1, y, c)
    across, twin = index(z, 1 - y, c), index(z, y, 1 - c)

    def arrived(owner):
        copy(0, owner, twin).wait_recv()

    def guarded(condition, act):
        pl.when(condition)(act)

    guarded(z < long - 1, lambda: copy(0, me, right, first_ref).start())
    guarded(z > 0, lambda: copy(1, me, left, first_ref).start())
    copy(2, me, across, first_ref).start()
    copy(3, me, twin, first_ref).start()

    def line_arrival(step):
        def from_left():
            owner = index(z - step, y, c)
            arrived(owner)
            guarded(z < long - 1, lambda: copy(0, owner, right).start())
            copy(2, owner, across).start()
            copy(3, owner, twin).start()

        def from_right():
            owner = index(z + step, y, c)
            arrived(owner)
            guarded(z > 0, lambda: copy(1, owner, left).start())
            copy(2, owner, across).start()
            copy(3, owner, twin).start()

        guarded(z - step >= 0, from_left)
        guarded(z + step <= long - 1, from_right)

    def across_arrival(step):
        def take(zz):
            owner = index(zz, 1 - y, c)
            arrived(owner)
            copy(3, owner, twin).start()

        if step == 0:
            take(z)
        else:
            guarded(z - step >= 0, lambda: take(z - step))
            guarded(z + step <= long - 1, lambda: take(z + step))

    for step in range(1, long):
        line_arrival(step)
        across_arrival(step - 1)
    across_arrival(long - 1)
    for zz in range(long):
        for yy in range(2):
            arrived(index(zz, yy, 1 - c))

    for zz in range(long):
        own = index(zz, y, c)
        guarded(jnp.logical_and(z < long - 1, zz <= z), lambda own=own: copy(0, own, right).wait_send())
        guarded(jnp.logical_and(z > 0, zz >= z), lambda own=own: copy(1, own, left).wait_send())
        copy(2, own, across).wait_send()
        copy(3, own, twin).wait_send()
        copy(3, index(zz, 1 - y, c), twin).wait_send()


def gather_kernel(n, own_ref, whole_ref, send_sem, recv_sem, local_sem):
    long = n // 4
    rows = own_ref.shape[1]
    z, y, c = position()
    greet(long, z, y, c)
    me = z * 4 + y * 2 + c
    local = pltpu.make_async_copy(
        own_ref,
        whole_ref.at[:, pl.ds(pl.multiple_of(me * rows, rows), rows), :],
        local_sem,
    )
    local.start()
    gather_steps(long, rows, z, y, c, whole_ref, own_ref, send_sem, recv_sem)
    local.wait()


def gather_rows(own, n, collective_id):
    layers, rows, width = own.shape
    return pl.pallas_call(
        functools.partial(gather_kernel, n),
        out_shape=jax.ShapeDtypeStruct((layers, n * rows, width), own.dtype),
        in_specs=[pl.BlockSpec(memory_space=pl.ANY)],
        out_specs=pl.BlockSpec(memory_space=pl.ANY),
        scratch_shapes=[
            pltpu.SemaphoreType.DMA((4, n)),
            pltpu.SemaphoreType.DMA((n,)),
            pltpu.SemaphoreType.DMA,
        ],
        compiler_params=pltpu.CompilerParams(
            collective_id=collective_id, has_side_effects=True, vmem_limit_bytes=VMEM_LIMIT
        ),
        name=f"gather_rows_{rows}",
    )(own)


def scatter_kernel(
    n, part_ref, sum_ref, core_buf, y_out, y_in, right_out, right_in, left_out, left_in,
    core_send, core_recv, y_send, y_recv, right_send, right_recv, left_send, left_recv,
):
    long = n // 4
    layers, rows, width = sum_ref.shape
    z, y, c = position()
    greet(long, z, y, c)
    f32 = jnp.float32

    def index(zz, yy, cc):
        return zz * 4 + yy * 2 + cc

    def rows_of(owner):
        return pl.ds(pl.multiple_of(owner * rows, rows), rows)

    def remote(src, dst, send, recv, target):
        return pltpu.make_async_remote_copy(
            src_ref=src, dst_ref=dst, send_sem=send, recv_sem=recv,
            device_id={"latent": target}, device_id_type=MESH,
        )

    order = []
    low, high = 0, long - 1
    while low <= high:
        order.append(high)
        if low < high:
            order.append(low)
        low, high = low + 1, high - 1
    pieces = [(zz, t) for zz in order for t in range(layers)]

    def core_copy(zz, side, t):
        owner = index(zz, 1 - y if side == 0 else y, 1 - c)
        return remote(
            part_ref.at[t, rows_of(owner), :], core_buf.at[side, zz, t],
            core_send.at[side, zz, t], core_recv.at[side, zz, t], index(z, y, 1 - c),
        )

    def y_copy(zz, t):
        return remote(
            y_out.at[zz, t], y_in.at[zz, t], y_send.at[zz, t], y_recv.at[zz, t],
            index(z, 1 - y, c),
        )

    def right_copy(zz, t):
        return remote(
            right_out.at[zz, t], right_in.at[zz, t], right_send.at[zz, t], right_recv.at[zz, t],
            index(z + 1, y, c),
        )

    def left_copy(zz, t):
        return remote(
            left_out.at[zz, t], left_in.at[zz, t], left_send.at[zz, t], left_recv.at[zz, t],
            index(z - 1, y, c),
        )

    for side in range(2):
        for zz, t in pieces:
            core_copy(zz, side, t).start()

    def start_y(piece):
        zz, t = piece
        core_copy(zz, 0, t).wait_recv()
        owner = index(zz, 1 - y, c)
        total = part_ref[t, rows_of(owner), :].astype(f32) + core_buf[0, zz, t].astype(f32)
        y_out[zz, t] = total.astype(y_out.dtype)
        y_copy(zz, t).start()

    ahead = 2
    for piece in pieces[:ahead]:
        start_y(piece)
    for number, (zz, t) in enumerate(pieces):
        core_copy(zz, 1, t).wait_recv()
        y_copy(zz, t).wait_recv()
        if number + ahead < len(pieces):
            start_y(pieces[number + ahead])

        def here(zz=zz, t=t):
            owner = index(zz, y, c)
            return (
                part_ref[t, rows_of(owner), :].astype(f32)
                + core_buf[1, zz, t].astype(f32)
                + y_in[zz, t].astype(f32)
            )

        @pl.when(zz == z)
        def _():
            sum_ref[t] = here()

        @pl.when(zz > z)
        def _():
            @pl.when(z == 0)
            def _():
                right_out[zz, t] = here().astype(right_out.dtype)

            @pl.when(z > 0)
            def _():
                right_copy(zz, t).wait_recv()
                right_out[zz, t] = (here() + right_in[zz, t].astype(f32)).astype(right_out.dtype)

            right_copy(zz, t).start()

        @pl.when(zz < z)
        def _():
            @pl.when(z == long - 1)
            def _():
                left_out[zz, t] = here().astype(left_out.dtype)

            @pl.when(z < long - 1)
            def _():
                left_copy(zz, t).wait_recv()
                left_out[zz, t] = (here() + left_in[zz, t].astype(f32)).astype(left_out.dtype)

            left_copy(zz, t).start()

    for t in range(layers):
        @pl.when(z > 0)
        def _():
            right_copy(z, t).wait_recv()
            sum_ref[t] += right_in[z, t].astype(f32)

        @pl.when(z < long - 1)
        def _():
            left_copy(z, t).wait_recv()
            sum_ref[t] += left_in[z, t].astype(f32)

    for zz, t in pieces:
        core_copy(zz, 0, t).wait_send()
        core_copy(zz, 1, t).wait_send()
        y_copy(zz, t).wait_send()
        pl.when(zz > z)(lambda zz=zz, t=t: right_copy(zz, t).wait_send())
        pl.when(zz < z)(lambda zz=zz, t=t: left_copy(zz, t).wait_send())


def scatter_sum(parts, n, collective_id):
    layers, all_rows, width = parts.shape
    rows, long = all_rows // n, n // 4
    line = pltpu.VMEM((long, layers, rows, width), parts.dtype)
    sems = pltpu.SemaphoreType.DMA((long, layers))
    two_sems = pltpu.SemaphoreType.DMA((2, long, layers))
    return pl.pallas_call(
        functools.partial(scatter_kernel, n),
        out_shape=jax.ShapeDtypeStruct((layers, rows, width), jnp.float32),
        in_specs=[pl.BlockSpec(memory_space=pltpu.VMEM)],
        out_specs=pl.BlockSpec(memory_space=pltpu.VMEM),
        scratch_shapes=[
            pltpu.VMEM((2, long, layers, rows, width), parts.dtype),
            line, line, line, line, line, line,
            two_sems, two_sems, sems, sems, sems, sems, sems, sems,
        ],
        compiler_params=pltpu.CompilerParams(
            collective_id=collective_id, has_side_effects=True, vmem_limit_bytes=VMEM_LIMIT
        ),
        name="scatter_sum",
    )(parts)


def plain_gather(own):
    return lax.all_gather(own, "latent", axis=1, tiled=True)


def body(n, row_store, row_slot, targets, enc_weight, enc_bias, dec_weight, dec_bias):
    layers = enc_weight.shape[0]
    row_count = row_slot.shape[0]
    own_rows = targets.shape[0]
    f32, bf16 = jnp.float32, jnp.bfloat16
    by_kernel = n % 4 == 0 and row_store.shape[0] % 16 == 0 and own_rows % 16 == 0

    store = jnp.transpose(row_store, (1, 0, 2))
    slots = gather_rows(store, n, 0) if by_kernel else plain_gather(store)
    slot_count = slots.shape[1]
    pick = row_slot[:, None] == jnp.arange(slot_count, dtype=row_slot.dtype)[None, :]
    slot_pre = jnp.concatenate(
        [
            jnp.dot(slots[source], enc_weight[source], preferred_element_type=f32)
            for source in range(layers)
        ],
        axis=1,
    )
    row_pre = jnp.dot(
        pick.astype(f32), slot_pre, precision=lax.Precision.HIGHEST, preferred_element_type=f32
    )
    wide = enc_weight.shape[2]
    pre_list = []
    latents = []
    for source in range(layers):
        pre_acts = row_pre[:, source * wide : (source + 1) * wide] + enc_bias[source][None, :]
        pre_list.append(pre_acts)
        latents.append(activate(pre_acts).astype(bf16))
    terms = [recon_terms(target, latents, dec_weight, layers) for target in range(layers)]
    if by_kernel:
        summed = scatter_sum(jnp.stack([term.astype(bf16) for term in terms], axis=0), n, 1)
    else:
        summed = lax.psum_scatter(
            jnp.stack(terms, axis=0), "latent", scatter_dimension=1, tiled=True
        )
    rebuilt = summed + dec_bias[:, None, :]
    factor = 1.0 / math.sqrt(row_count)
    wanted = jnp.transpose(targets, (1, 0, 2)).astype(f32)
    error_part = ((rebuilt - wanted) * factor).astype(bf16)
    errors = gather_rows(error_part, n, 2) if by_kernel else plain_gather(error_part)
    grad_dec_list = []
    for source in range(layers):
        for target in range(source, layers):
            grad_dec_list.append(
                jnp.dot(latents[source].T, errors[target], preferred_element_type=f32).astype(bf16)
            )
    grad_dec = jnp.stack(grad_dec_list, axis=0)
    grad_dbias = jnp.sum(errors.astype(f32), axis=1)
    grad_ebias_list = []
    low_list = []
    for source in range(layers):
        back = None
        for target in range(source, layers):
            product = lax.dot_general(
                errors[target],
                dec_weight[pair_index(source, target, layers)],
                (((1,), (1,)), ((), ())),
                preferred_element_type=f32,
            )
            back = product if back is None else back + product
        unused, pullback = jax.vjp(activate, pre_list[source])
        dpre = pullback(back)[0]
        grad_ebias_list.append(jnp.sum(dpre, axis=0))
        low_list.append(dpre.astype(bf16))
    slot_dpre = lax.dot_general(
        pick.astype(bf16),
        jnp.concatenate(low_list, axis=1),
        (((0,), (0,)), ((), ())),
        preferred_element_type=f32,
    ).astype(bf16)
    grad_enc = jnp.stack(
        [
            lax.dot_general(
                slots[source],
                slot_dpre[:, source * wide : (source + 1) * wide],
                (((0,), (0,)), ((), ())),
                preferred_element_type=f32,
            ).astype(bf16)
            for source in range(layers)
        ],
        axis=0,
    )
    grad_ebias = jnp.stack(grad_ebias_list, axis=0)
    return (jnp.transpose(rebuilt, (1, 0, 2)), grad_enc, grad_ebias, grad_dec, grad_dbias)


def solution(mesh):
    in_specs = (
        P(("groups", "latent"), None, None),
        P("groups"),
        P(("groups", "latent"), None, None),
        P("groups", None, "latent"),
        P("groups", "latent"),
        P("groups", "latent", None),
        P("groups", None),
    )
    out_specs = (
        P(("groups", "latent"), None, None),
        P("groups", None, "latent"),
        P("groups", "latent"),
        P("groups", "latent", None),
        P("groups", None),
    )
    return jax.shard_map(
        functools.partial(body, mesh.shape["latent"]),
        mesh=mesh,
        in_specs=in_specs,
        out_specs=out_specs,
        check_vma=False,
    )
```

time: 333 us -> 175 us (0.53)
  waiting for transfers between devices: 246 us -> 0 us
  Pallas kernels: 0 us -> 137 us
  local copies, waits for them, and re-layouts: 35.3 us -> 6.45 us
  between operations: 14 us -> 0.89 us
  other arithmetic: 22.4 us -> 11.3 us
  matrix products: 14.3 us -> 19.7 us
    pallas_call x0 -> x3, Pallas kernels: none -> 137 us  [the longest x2 99.8 us: gather_rows(): pl.pallas_call(functools.partial(gather_kernel, n), out_shape=jax.ShapeDt...]
    all_gather x2 -> x0, waiting for transfers between devices: 136 us -> none  [the longest x1 84.4 us: body(): gathered = lax.all_gather(row_store, 'latent', axis=0, tiled=True)]
    reduce_scatter x1 -> x0, waiting for transfers between devices: 110 us -> none  [body(): lax.psum_scatter(stacked, 'latent', scatter_dimension=0, tiled=True)]
    gather x1 -> x0, local copies, waits for them, and re-layouts: 19.2 us -> none  [body(): inputs = jnp.take(gathered, row_slot, axis=0)]
    slice x1 -> x0, local copies, waits for them, and re-layouts: 9.82 us -> none  [body(): inputs[:, source]]
    select_n x2 -> x0, other arithmetic: 9.7 us -> none  [body(): inputs = jnp.take(gathered, row_slot, axis=0)]
    dot_general x13 -> x15, matrix products: 14.3 us -> 19.7 us  [the longest x2 7.57 us: body(): jnp.dot(slots[source], enc_weight[source], preferred_element_type=f32)]
  transfers between devices with their start and end apart: 3 -> 0, of which waited for: 3 -> 0; matrix products, arithmetic and copies ran while one was open for 1% -> 0% of each run, Pallas kernels for 0% -> 0%
where the time goes in v1:
time: 175 us
  Pallas kernels  137 us (78%)
  matrix products  19.7 us (11%)
  other arithmetic  11.3 us (6%)
  local copies, waits for them, and re-layouts  6.45 us (4%)
    pallas_call x2, Pallas kernels, gather_rows(): pl.pallas_call(functools.partial(gather_kernel, n), out_shape=jax.ShapeDt...  99.8 us
    pallas_call x1, Pallas kernels, scatter_sum(): pl.pallas_call(functools.partial(scatter_kernel, n), out_shape=jax.ShapeD...  37 us
    dot_general x2, matrix products, body(): jnp.dot(slots[source], enc_weight[source], preferred_element_type=f32)  7.57 us
    unnamed x25, local copies, waits for them, and re-layouts  5.69 us
    dot_general x3, matrix products, body(): jnp.dot(latents[source].T, errors[target], preferred_element_type=f32)  4.93 us
    reduce_sum x1, other arithmetic, body(): grad_dbias = jnp.sum(errors.astype(f32), axis=1)  3.91 us

profile of v1, /device:TPU:0, one launch (start us, length us, event | category | flops | bytes accessed | tf_op | source)
XLA Modules:
  0.0 175.1 jit_solution(5487734204057188612)
XLA Ops:
  0.6 0.8 slice_bitcast_fusion
  1.4 1.9 %copy.18 = bf16[32,2,4608]{2,0,1:T(8,128)(2,1)} copy(bf16[32,2,4608]{2,1,0:T(2,128)(2,1)} %param.7) | data formatting | bytes 1179648 | tf_op args[0]
  3.3 62.7 %gather_rows_32.1 = bf16[2,512,4608]{2,1,0:T(8,128)(2,1)} custom-call(bf16[2,32,4608]{2,1,0:T(8,128)(2,1)} %bitcast.106), custom_call_target="tpu_custom_call" | custom-call | tf_op jit(solution)/shard_map/gather_rows_32/pallas_call | solution.py:160
  66.0 3.7 %fusion.9 = f32[512,128]{1,0:T(8,128)S(1)} fusion(bf16[2,512,4608]{2,1,0:T(8,128)(2,1)} %gather_rows_32.1, bf16[2,4608,128]{2,1,0:T(8,128)(2,1)S(1)} %copy-done.7), kind=kOutput, calls=%fused_computation.18 | convolution fusion | flops 603979776 | bytes 6160384 | tf_op jit(solution)/shard_map/dot_general | solution.py:351
  69.7 0.0 copy-start.6
  69.7 0.0 copy-start.1
  69.8 3.9 %fusion.12 = f32[512,128]{1,0:T(8,128)S(1)} fusion(bf16[2,512,4608]{2,1,0:T(8,128)(2,1)} %gather_rows_32.1, bf16[2,4608,128]{2,1,0:T(8,128)(2,1)S(1)} %copy-done.7), kind=kOutput, calls=%fused_computation.21 | convolution fusion | flops 603979776 | bytes 6160384 | tf_op jit(solution)/shard_map/dot_general | solution.py:351
  73.6 0.5 fusion.57
  74.1 0.1 multiply_convert_fusion.1
  74.2 0.0 copy-start.2
  74.2 0.8 fusion.2
  75.0 0.8 fusion.36
  75.7 0.8 fusion.1
  76.5 2.6 %pad_maximum_fusion.part_ref = bf16[2,256,4608]{2,1,0:T(8,128)(2,1)} fusion(bf16[1,256,4608]{2,1,0:T(8,128)(2,1)S(1)} %fusion.1, bf16[1,256,4608]{2,1,0:T(8,128)(2,1)S(1)} %fusion.2), kind=kLoop, calls=%fused_computation.16 | loop fusion | flops 2359296 | bytes 9437184 | tf_op jit(solution)/shard_map/stack | solution.py:368
  79.2 37.0 %scatter_sum.1 = f32[2,16,4608]{2,1,0:T(8,128)} custom-call(bf16[2,256,4608]{2,1,0:T(8,128)(2,1)} %pad_maximum_fusion.part_ref), custom_call_target="tpu_custom_call" | custom-call | tf_op jit(solution)/shard_map/scatter_sum/pallas_call | solution.py:317
  116.2 1.9 %fusion.56 = (bf16[2,16,4608]{2,1,0:T(8,128)(2,1)}, f32[16,2,4608]{2,0,1:T(8,128)S(1)}) fusion(f32[2,16,4608]{2,1,0:T(8,128)} %scatter_sum.1, bf16[16,2,4608]{2,1,0:T(2,128)(2,1)S(1)} %copy-done.4, f32[2,4608]{1,0:T(2,128)S(1)} %copy-done.5), kind=kLoop, calls=%fused_computation.65 | loop fusion | flops 737280 | bytes 1806336 | tf_op jit(solution)/shard_map/convert_element_type | solution.py:376
  118.1 1.3 copy.14
  119.4 37.1 %gather_rows_16.1 = bf16[2,256,4608]{2,1,0:T(8,128)(2,1)} custom-call(bf16[2,16,4608]{2,1,0:T(8,128)(2,1)} %get-tuple-element.10.own_ref), custom_call_target="tpu_custom_call" | custom-call | tf_op jit(solution)/shard_map/gather_rows_16/pallas_call | solution.py:160
  156.5 3.9 %convert_reduce_fusion = f32[2,4608]{1,0:T(2,128)} fusion(bf16[2,256,4608]{2,1,0:T(8,128)(2,1)} %gather_rows_16.1), kind=kLoop, calls=%fused_computation | loop fusion | flops 4709376 | bytes 4755456 | tf_op jit(solution)/shard_map/reduce_sum | solution.py:385
  160.4 0.8 fusion.91
  161.2 0.8 fusion.22
  162.0 0.8 fusion.90
  162.8 0.6 pad_maximum_fusion.3
  163.4 0.4 convolution_convert_fusion.6
  163.8 0.5 fusion.7
  164.4 0.8 fusion.4
  165.2 0.8 fusion.3
  166.0 0.2 pad_maximum_fusion.2
  166.3 2.4 %copy.15 = bf16[2,4608,128]{2,1,0:T(8,128)(2,1)} copy(bf16[2,4608,128]{1,2,0:T(8,128)(2,1)S(1)} %pad_maximum_fusion.2) | data formatting | bytes 4718592
  168.7 2.2 %fusion.6 = bf16[1,128,4608]{2,1,0:T(8,128)(2,1)S(1)} fusion(bf16[256,128]{1,0:T(8,128)(2,1)} %copy-done.2, bf16[2,256,4608]{2,1,0:T(8,128)(2,1)} %gather_rows_16.1), kind=kOutput, calls=%fused_computation.14 | convolution fusion | flops 302579712 | bytes 3604480 | tf_op jit(solution)/shard_map/dot_general | solution.py:382
  170.9 2.2 %fusion.5 = bf16[1,128,4608]{2,1,0:T(8,128)(2,1)S(1)} fusion(bf16[256,128]{1,0:T(8,128)(2,1)S(1)} %copy-done.3, bf16[2,256,4608]{2,1,0:T(8,128)(2,1)} %gather_rows_16.1), kind=kOutput, calls=%fused_computation.13 | convolution fusion | flops 302579712 | bytes 3604480 | tf_op jit(solution)/shard_map/dot_general | solution.py:382
  173.1 2.0 %pad_maximum_fusion.1 = bf16[3,128,4608]{2,1,0:T(8,128)(2,1)} fusion(bf16[1,128,4608]{2,1,0:T(8,128)(2,1)S(1)} %fusion.7, bf16[1,128,4608]{2,1,0:T(8,128)(2,1)S(1)} %fusion.6, bf16[1,128,4608]{2,1,0:T(8,128)(2,1)S(1)} %fusion.5), kind=kLoop, calls=%fused_computation.27 | loop fusion | flops 3538944 | bytes 7077888 | tf_op jit(solution)/shard_map/stack | solution.py:384
  (20 shorter events, 0.0 us)
Async XLA Ops:
  3.3 62.7 %copy-start.7 = (bf16[2,4608,128]{2,1,0:T(8,128)(2,1)S(1)}, bf16[2,4608,128]{2,1,0:T(8,128)(2,1)}, u32[]{:S(2)}) copy-start(bf16[2,4608,128]{2,1,0:T(8,128)(2,1)} %param.10) | copy-start | bytes 7077892
  69.7 3.9 %copy-start.6 = (s32[256]{0:T(256)S(1)}, s32[256]{0:T(256)}, u32[]{:S(2)}) copy-start(s32[256]{0:T(256)} %param.8) | copy-start | bytes 3076
  69.7 4.4 %copy-start.1 = (bf16[3,128,4608]{2,1,0:T(8,128)(2,1)S(1)}, bf16[3,128,4608]{2,1,0:T(8,128)(2,1)}, u32[]{:S(2)}) copy-start(bf16[3,128,4608]{2,1,0:T(8,128)(2,1)} %param.12) | copy-start | bytes 10616836
  74.2 0.8 copy-start.2
  79.2 37.0 %copy-start.4 = (bf16[16,2,4608]{2,1,0:T(2,128)(2,1)S(1)}, bf16[16,2,4608]{2,1,0:T(2,128)(2,1)}, u32[]{:S(2)}) copy-start(bf16[16,2,4608]{2,1,0:T(2,128)(2,1)} %param.9) | copy-start | bytes 884740
  79.2 37.0 %copy-start.5 = (f32[2,4608]{1,0:T(2,128)S(1)}, f32[2,4608]{1,0:T(2,128)}, u32[]{:S(2)}) copy-start(f32[2,4608]{1,0:T(2,128)} %param.13) | copy-start | bytes 110596
  156.5 3.9 %copy-start = (bf16[2,256,4608]{2,1,0:T(8,128)(2,1)S(1)}, bf16[2,256,4608]{2,1,0:T(8,128)(2,1)}, u32[]{:S(2)}) copy-start(bf16[2,256,4608]{2,1,0:T(8,128)(2,1)} %gather_rows_16.1) | copy-start | bytes 14155780
  156.5 7.8 %slice-start = ((s8[9437184]{0:T(1024)(128)(4,1)}), s8[4194304]{0:T(1024)(128)(4,1)S(1)}, s32[]{:S(2)}) async-start(s8[9437184]{0:T(1024)(128)(4,1)} %bitcast.104), calls=%async_computation | async-start | bytes 8388608
  160.4 3.9 %slice-start.1 = ((s8[9437184]{0:T(1024)(128)(4,1)}), s8[4194304]{0:T(1024)(128)(4,1)S(1)}, s32[]{:S(2)}) async-start(s8[9437184]{0:T(1024)(128)(4,1)} %bitcast.104), calls=%async_computation.1 | async-start | bytes 8388608
  162.0 2.4 %slice-start.2 = ((s8[9437184]{0:T(1024)(128)(4,1)}), s8[1048576]{0:T(1024)(128)(4,1)S(1)}, s32[]{:S(2)}) async-start(s8[9437184]{0:T(1024)(128)(4,1)} %bitcast.104), calls=%async_computation.2 | async-start | bytes 2097152
  168.7 2.2 %copy-start.3 = (bf16[256,128]{1,0:T(8,128)(2,1)S(1)}, bf16[256,128]{1,0:T(8,128)(2,1)}, u32[]{:S(2)}) copy-start(bf16[256,128]{1,0:T(8,128)(2,1)} %copy-done.2) | copy-start | bytes 196612

commit v2 on v1

--- a/solution.py
+++ b/solution.py
@@ -60,98 +60,136 @@
     pl.semaphore_wait(barrier, peers)
 
 
-def gather_steps(long, rows, z, y, c, whole, first_ref, send_sem, recv_sem):
-    def index(zz, yy, cc):
+class Gather:
+    def __init__(self, long, z, y, c, views, routes, firsts, send_sem, recv_sem):
+        self.long, self.z, self.y, self.c = long, z, y, c
+        self.views, self.routes, self.firsts = views, routes, firsts
+        self.send_sem, self.recv_sem = send_sem, recv_sem
+        self.me = self.index(z, y, c)
+        self.targets = (
+            self.index(z + 1, y, c), self.index(z - 1, y, c),
+            self.index(z, 1 - y, c), self.index(z, y, 1 - c),
+        )
+
+    def index(self, zz, yy, cc):
         return zz * 4 + yy * 2 + cc
 
-    def block(owner):
-        return whole.at[:, pl.ds(pl.multiple_of(owner * rows, rows), rows), :]
-
-    def copy(kind, owner, target, src=None):
+    def copy(self, part, kind, owner, src=None):
+        view = self.views[part](owner)
         return pltpu.make_async_remote_copy(
-            src_ref=block(owner) if src is None else src,
-            dst_ref=block(owner),
-            send_sem=send_sem.at[kind, owner],
-            recv_sem=recv_sem.at[owner],
-            device_id={"latent": target},
+            src_ref=view if src is None else src,
+            dst_ref=view,
+            send_sem=self.send_sem.at[part, kind, owner],
+            recv_sem=self.recv_sem.at[part, owner],
+            device_id={"latent": self.targets[kind]},
             device_id_type=MESH,
         )
 
-    me = index(z, y, c)
-    left, right = index(z - 1, y, c), index(z + 1, y, c)
-    across, twin = index(z, 1 - y, c), index(z, y, 1 - c)
-
-    def arrived(owner):
-        copy(0, owner, twin).wait_recv()
-
-    def guarded(condition, act):
-        pl.when(condition)(act)
-
-    guarded(z < long - 1, lambda: copy(0, me, right, first_ref).start())
-    guarded(z > 0, lambda: copy(1, me, left, first_ref).start())
-    copy(2, me, across, first_ref).start()
-    copy(3, me, twin, first_ref).start()
-
-    def line_arrival(step):
-        def from_left():
-            owner = index(z - step, y, c)
-            arrived(owner)
-            guarded(z < long - 1, lambda: copy(0, owner, right).start())
-            copy(2, owner, across).start()
-            copy(3, owner, twin).start()
-
-        def from_right():
-            owner = index(z + step, y, c)
-            arrived(owner)
-            guarded(z > 0, lambda: copy(1, owner, left).start())
-            copy(2, owner, across).start()
-            copy(3, owner, twin).start()
-
-        guarded(z - step >= 0, from_left)
-        guarded(z + step <= long - 1, from_right)
-
-    def across_arrival(step):
+    def arrived(self, part, owner):
+        self.copy(part, 3, owner).wait_recv()
+
+    def sideways(self, part, owner, src=None):
+        pl.when(self.z < self.long - 1)(lambda: self.copy(part, 0, owner, src).start())
+        pl.when(self.z > 0)(lambda: self.copy(part, 1, owner, src).start())
+
+    def begin(self, part):
+        src = self.firsts[part]
+        if self.routes[part] == 1:
+            self.copy(part, 2, self.me, src).start()
+            self.sideways(part, self.me, src)
+        else:
+            self.sideways(part, self.me, src)
+            self.copy(part, 2, self.me, src).start()
+        self.copy(part, 3, self.me, src).start()
+
+    def line(self, part, step):
+        z, y, c, long = self.z, self.y, self.c, self.long
+        sides = (y,) if self.routes[part] == 0 else (y, 1 - y)
+
+        def take(zz, kind, inside):
+            for side in sides:
+                owner = self.index(zz, side, c)
+                self.arrived(part, owner)
+                pl.when(inside)(lambda owner=owner: self.copy(part, kind, owner).start())
+                if self.routes[part] == 0:
+                    self.copy(part, 2, owner).start()
+                self.copy(part, 3, owner).start()
+
+        pl.when(z - step >= 0)(lambda: take(z - step, 0, z < long - 1))
+        pl.when(z + step <= long - 1)(lambda: take(z + step, 1, z > 0))
+
+    def across(self, part, step):
+        z, y, c, long = self.z, self.y, self.c, self.long
+
         def take(zz):
-            owner = index(zz, 1 - y, c)
-            arrived(owner)
-            copy(3, owner, twin).start()
+            owner = self.index(zz, 1 - y, c)
+            self.arrived(part, owner)
+            if self.routes[part] == 1:
+                self.sideways(part, owner)
+            self.copy(part, 3, owner).start()
 
         if step == 0:
             take(z)
-        else:
-            guarded(z - step >= 0, lambda: take(z - step))
-            guarded(z + step <= long - 1, lambda: take(z + step))
-
-    for step in range(1, long):
-        line_arrival(step)
-        across_arrival(step - 1)
-    across_arrival(long - 1)
-    for zz in range(long):
-        for yy in range(2):
-            arrived(index(zz, yy, 1 - c))
-
-    for zz in range(long):
-        own = index(zz, y, c)
-        guarded(jnp.logical_and(z < long - 1, zz <= z), lambda own=own: copy(0, own, right).wait_send())
-        guarded(jnp.logical_and(z > 0, zz >= z), lambda own=own: copy(1, own, left).wait_send())
-        copy(2, own, across).wait_send()
-        copy(3, own, twin).wait_send()
-        copy(3, index(zz, 1 - y, c), twin).wait_send()
+        elif self.routes[part] == 0:
+            pl.when(z - step >= 0)(lambda: take(z - step))
+            pl.when(z + step <= long - 1)(lambda: take(z + step))
+
+    def finish(self, part):
+        z, y, c, long = self.z, self.y, self.c, self.long
+        for zz in range(long):
+            for yy in range(2):
+                self.arrived(part, self.index(zz, yy, 1 - c))
+        for zz in range(long):
+            for side in (y, 1 - y):
+                owner = self.index(zz, side, c)
+                self.copy(part, 3, owner).wait_send()
+                if side is y or self.routes[part] == 1:
+                    pl.when(jnp.logical_and(z < long - 1, zz <= z))(
+                        lambda owner=owner: self.copy(part, 0, owner).wait_send()
+                    )
+                    pl.when(jnp.logical_and(z > 0, zz >= z))(
+                        lambda owner=owner: self.copy(part, 1, owner).wait_send()
+                    )
+            if self.routes[part] == 0:
+                self.copy(part, 2, self.index(zz, y, c)).wait_send()
+        if self.routes[part] == 1:
+            self.copy(part, 2, self.me).wait_send()
+
+
+def column_cuts(width, share):
+    cut = int(width * share) // 128 * 128
+    return (pl.ds(0, cut), pl.ds(cut, width - cut))
+
+
+def rows_of(owner, rows):
+    return pl.ds(pl.multiple_of(owner * rows, rows), rows)
 
 
 def gather_kernel(n, own_ref, whole_ref, send_sem, recv_sem, local_sem):
     long = n // 4
-    rows = own_ref.shape[1]
+    layers, rows, width = own_ref.shape
     z, y, c = position()
     greet(long, z, y, c)
-    me = z * 4 + y * 2 + c
+    cuts = column_cuts(width, 5 / 6)
+    views = [
+        lambda owner, cut=cut: whole_ref.at[:, rows_of(owner, rows), cut] for cut in cuts
+    ]
+    firsts = [own_ref.at[:, :, cut] for cut in cuts]
+    gather = Gather(long, z, y, c, views, (0, 1), firsts, send_sem, recv_sem)
     local = pltpu.make_async_copy(
-        own_ref,
-        whole_ref.at[:, pl.ds(pl.multiple_of(me * rows, rows), rows), :],
-        local_sem,
+        own_ref, whole_ref.at[:, rows_of(gather.me, rows), :], local_sem
     )
     local.start()
-    gather_steps(long, rows, z, y, c, whole_ref, own_ref, send_sem, recv_sem)
+    gather.begin(1)
+    gather.begin(0)
+    gather.across(1, 0)
+    for step in range(1, long):
+        gather.line(0, step)
+        gather.line(1, step)
+        gather.across(0, step - 1)
+    gather.across(0, long - 1)
+    gather.finish(0)
+    gather.finish(1)
     local.wait()
 
 
@@ -163,20 +201,22 @@
         in_specs=[pl.BlockSpec(memory_space=pl.ANY)],
         out_specs=pl.BlockSpec(memory_space=pl.ANY),
         scratch_shapes=[
-            pltpu.SemaphoreType.DMA((4, n)),
-            pltpu.SemaphoreType.DMA((n,)),
+            pltpu.SemaphoreType.DMA((2, 4, n)),
+            pltpu.SemaphoreType.DMA((2, n)),
             pltpu.SemaphoreType.DMA,
         ],
         compiler_params=pltpu.CompilerParams(
             collective_id=collective_id, has_side_effects=True, vmem_limit_bytes=VMEM_LIMIT
         ),
-        name=f"gather_rows_{rows}",
+        name="gather_rows",
     )(own)
 
 
-def scatter_kernel(
-    n, part_ref, sum_ref, core_buf, y_out, y_in, right_out, right_in, left_out, left_in,
+def exchange_kernel(
+    n, factor, part_ref, bias_ref, wanted_ref, sum_ref, whole_ref,
+    own_error, core_buf, y_out, y_in, right_out, right_in, left_out, left_in,
     core_send, core_recv, y_send, y_recv, right_send, right_recv, left_send, left_recv,
+    send_sem, recv_sem, local_sem,
 ):
     long = n // 4
     layers, rows, width = sum_ref.shape
@@ -186,9 +226,6 @@
 
     def index(zz, yy, cc):
         return zz * 4 + yy * 2 + cc
-
-    def rows_of(owner):
-        return pl.ds(pl.multiple_of(owner * rows, rows), rows)
 
     def remote(src, dst, send, recv, target):
         return pltpu.make_async_remote_copy(
@@ -203,12 +240,12 @@
         if low < high:
             order.append(low)
         low, high = low + 1, high - 1
-    pieces = [(zz, t) for zz in order for t in range(layers)]
+    pieces = [(zz, t) for t in range(layers) for zz in order]
 
     def core_copy(zz, side, t):
         owner = index(zz, 1 - y if side == 0 else y, 1 - c)
         return remote(
-            part_ref.at[t, rows_of(owner), :], core_buf.at[side, zz, t],
+            part_ref.at[t, rows_of(owner, rows), :], core_buf.at[side, zz, t],
             core_send.at[side, zz, t], core_recv.at[side, zz, t], index(z, y, 1 - c),
         )
 
@@ -230,38 +267,38 @@
             index(z - 1, y, c),
         )
 
-    for side in range(2):
-        for zz, t in pieces:
+    for zz, t in pieces:
+        for side in range(2):
             core_copy(zz, side, t).start()
 
     def start_y(piece):
         zz, t = piece
         core_copy(zz, 0, t).wait_recv()
         owner = index(zz, 1 - y, c)
-        total = part_ref[t, rows_of(owner), :].astype(f32) + core_buf[0, zz, t].astype(f32)
+        total = part_ref[t, rows_of(owner, rows), :].astype(f32) + core_buf[0, zz, t].astype(f32)
         y_out[zz, t] = total.astype(y_out.dtype)
         y_copy(zz, t).start()
 
-    ahead = 2
-    for piece in pieces[:ahead]:
-        start_y(piece)
-    for number, (zz, t) in enumerate(pieces):
+    ahead = min(3, len(pieces))
+
+    def sum_piece(number):
+        zz, t = pieces[number]
         core_copy(zz, 1, t).wait_recv()
         y_copy(zz, t).wait_recv()
         if number + ahead < len(pieces):
             start_y(pieces[number + ahead])
 
-        def here(zz=zz, t=t):
+        def here():
             owner = index(zz, y, c)
             return (
-                part_ref[t, rows_of(owner), :].astype(f32)
+                part_ref[t, rows_of(owner, rows), :].astype(f32)
                 + core_buf[1, zz, t].astype(f32)
                 + y_in[zz, t].astype(f32)
             )
 
         @pl.when(zz == z)
         def _():
-            sum_ref[t] = here()
+            sum_ref[t] = here() + bias_ref[pl.ds(t, 1), :]
 
         @pl.when(zz > z)
         def _():
@@ -289,7 +326,24 @@
 
             left_copy(zz, t).start()
 
+    cuts = column_cuts(width, 2 / 3)
+    views, firsts = [], []
     for t in range(layers):
+        for cut in cuts:
+            views.append(
+                lambda owner, t=t, cut=cut: whole_ref.at[t, rows_of(owner, rows), cut]
+            )
+            firsts.append(own_error.at[t, :, cut])
+    gather = Gather(
+        long, z, y, c, views, (0, 1) * layers, firsts, send_sem, recv_sem
+    )
+
+    def local(t):
+        return pltpu.make_async_copy(
+            own_error.at[t], whole_ref.at[t, rows_of(gather.me, rows), :], local_sem.at[t]
+        )
+
+    def close(t):
         @pl.when(z > 0)
         def _():
             right_copy(z, t).wait_recv()
@@ -299,6 +353,33 @@
         def _():
             left_copy(z, t).wait_recv()
             sum_ref[t] += left_in[z, t].astype(f32)
+
+        own_error[t] = ((sum_ref[t] - wanted_ref[t].astype(f32)) * factor).astype(own_error.dtype)
+        local(t).start()
+        gather.begin(2 * t + 1)
+        gather.begin(2 * t)
+
+    def spread_step(t, step):
+        gather.line(2 * t, step)
+        if step == 1:
+            gather.across(2 * t + 1, 0)
+        gather.line(2 * t + 1, step)
+
+    for piece in pieces[:ahead]:
+        start_y(piece)
+    for t in range(layers):
+        for number in range(long):
+            sum_piece(t * long + number)
+            if t > 0 and number > 0:
+                spread_step(t - 1, number)
+        close(t)
+        if t > 0:
+            for step in range(long):
+                gather.across(2 * (t - 1), step)
+    for step in range(1, long):
+        spread_step(layers - 1, step)
+        gather.across(2 * (layers - 1), step - 1)
+    gather.across(2 * (layers - 1), long - 1)
 
     for zz, t in pieces:
         core_copy(zz, 0, t).wait_send()
@@ -306,29 +387,41 @@
         y_copy(zz, t).wait_send()
         pl.when(zz > z)(lambda zz=zz, t=t: right_copy(zz, t).wait_send())
         pl.when(zz < z)(lambda zz=zz, t=t: left_copy(zz, t).wait_send())
-
-
-def scatter_sum(parts, n, collective_id):
+    for t in range(layers):
+        gather.finish(2 * t)
+        gather.finish(2 * t + 1)
+        local(t).wait()
+
+
+def exchange(parts, bias, wanted, factor, n, collective_id):
     layers, all_rows, width = parts.shape
     rows, long = all_rows // n, n // 4
     line = pltpu.VMEM((long, layers, rows, width), parts.dtype)
     sems = pltpu.SemaphoreType.DMA((long, layers))
     two_sems = pltpu.SemaphoreType.DMA((2, long, layers))
+    vmem = pl.BlockSpec(memory_space=pltpu.VMEM)
     return pl.pallas_call(
-        functools.partial(scatter_kernel, n),
-        out_shape=jax.ShapeDtypeStruct((layers, rows, width), jnp.float32),
-        in_specs=[pl.BlockSpec(memory_space=pltpu.VMEM)],
-        out_specs=pl.BlockSpec(memory_space=pltpu.VMEM),
+        functools.partial(exchange_kernel, n, factor),
+        out_shape=(
+            jax.ShapeDtypeStruct((layers, rows, width), jnp.float32),
+            jax.ShapeDtypeStruct((layers, all_rows, width), parts.dtype),
+        ),
+        in_specs=[vmem, vmem, vmem],
+        out_specs=(vmem, pl.BlockSpec(memory_space=pl.ANY)),
         scratch_shapes=[
+            pltpu.VMEM((layers, rows, width), parts.dtype),
             pltpu.VMEM((2, long, layers, rows, width), parts.dtype),
             line, line, line, line, line, line,
             two_sems, two_sems, sems, sems, sems, sems, sems, sems,
+            pltpu.SemaphoreType.DMA((2 * layers, 4, n)),
+            pltpu.SemaphoreType.DMA((2 * layers, n)),
+            pltpu.SemaphoreType.DMA((layers,)),
         ],
         compiler_params=pltpu.CompilerParams(
             collective_id=collective_id, has_side_effects=True, vmem_limit_bytes=VMEM_LIMIT
         ),
-        name="scatter_sum",
-    )(parts)
+        name="exchange",
+    )(parts, bias, wanted)
 
 
 def plain_gather(own):
@@ -364,17 +457,17 @@
         pre_list.append(pre_acts)
         latents.append(activate(pre_acts).astype(bf16))
     terms = [recon_terms(target, latents, dec_weight, layers) for target in range(layers)]
+    factor = 1.0 / math.sqrt(row_count)
+    wanted = jnp.transpose(targets, (1, 0, 2))
     if by_kernel:
-        summed = scatter_sum(jnp.stack([term.astype(bf16) for term in terms], axis=0), n, 1)
+        parts = jnp.stack([term.astype(bf16) for term in terms], axis=0)
+        rebuilt, errors = exchange(parts, dec_bias, wanted, factor, n, 1)
     else:
         summed = lax.psum_scatter(
             jnp.stack(terms, axis=0), "latent", scatter_dimension=1, tiled=True
         )
-    rebuilt = summed + dec_bias[:, None, :]
-    factor = 1.0 / math.sqrt(row_count)
-    wanted = jnp.transpose(targets, (1, 0, 2)).astype(f32)
-    error_part = ((rebuilt - wanted) * factor).astype(bf16)
-    errors = gather_rows(error_part, n, 2) if by_kernel else plain_gather(error_part)
+        rebuilt = summed + dec_bias[:, None, :]
+        errors = plain_gather(((rebuilt - wanted.astype(f32)) * factor).astype(bf16))
     grad_dec_list = []
     for source in range(layers):
         for target in range(source, layers):

time: 175 us -> 181 us (1.034)
  Pallas kernels: 137 us -> 142 us
  local copies, waits for them, and re-layouts: 6.45 us -> 9.36 us
  other arithmetic: 11.3 us -> 9.24 us
    pallas_call x1, Pallas kernels: 37 us -> 82 us  [exchange(): pl.pallas_call(functools.partial(exchange_kernel, n, factor), out_shape=(...]
    pallas_call x2 -> x1, Pallas kernels: 99.8 us -> 59.6 us  [gather_rows(): pl.pallas_call(functools.partial(gather_kernel, n), out_shape=jax.ShapeDt...]
    unnamed x25 -> x22, local copies, waits for them, and re-layouts: 5.69 us -> 8.6 us
    convert_element_type x1 -> x0, other arithmetic: 1.87 us -> none  [body(): error_part = ((rebuilt - wanted) * factor).astype(bf16)]
where the time goes in v2:
time: 181 us
  Pallas kernels  142 us (78%)
  matrix products  19.7 us (11%)
  local copies, waits for them, and re-layouts  9.36 us (5%)
  other arithmetic  9.24 us (5%)
    pallas_call x1, Pallas kernels, exchange(): pl.pallas_call(functools.partial(exchange_kernel, n, factor), out_shape=(...  82 us
    pallas_call x1, Pallas kernels, gather_rows(): pl.pallas_call(functools.partial(gather_kernel, n), out_shape=jax.ShapeDt...  59.6 us
    unnamed x22, local copies, waits for them, and re-layouts  8.6 us
    dot_general x2, matrix products, body(): jnp.dot(slots[source], enc_weight[source], preferred_element_type=f32)  7.57 us
    dot_general x3, matrix products, body(): jnp.dot(latents[source].T, errors[target], preferred_element_type=f32)  4.93 us
    reduce_sum x1, other arithmetic, body(): grad_dbias = jnp.sum(errors.astype(f32), axis=1)  3.85 us

profile of v2, /device:TPU:0, one launch (start us, length us, event | category | flops | bytes accessed | tf_op | source)
XLA Modules:
  0.0 180.7 jit_solution(17226467885631155165)
XLA Ops:
  0.6 0.8 slice_bitcast_fusion
  1.4 1.7 copy.19
  3.1 1.9 %copy.18 = bf16[32,2,4608]{2,0,1:T(8,128)(2,1)} copy(bf16[32,2,4608]{2,1,0:T(2,128)(2,1)} %param.7) | data formatting | bytes 1179648 | tf_op args[0]
  5.0 59.6 %gather_rows.1 = bf16[2,512,4608]{2,1,0:T(8,128)(2,1)} custom-call(bf16[2,32,4608]{2,1,0:T(8,128)(2,1)} %bitcast.102), custom_call_target="tpu_custom_call" | custom-call | tf_op jit(solution)/shard_map/gather_rows/pallas_call | solution.py:198
  64.7 3.7 %fusion.9 = f32[512,128]{1,0:T(8,128)S(1)} fusion(bf16[2,512,4608]{2,1,0:T(8,128)(2,1)} %gather_rows.1, bf16[2,4608,128]{2,1,0:T(8,128)(2,1)S(1)} %copy-done.5), kind=kOutput, calls=%fused_computation.18 | convolution fusion | flops 603979776 | bytes 6160384 | tf_op jit(solution)/shard_map/dot_general | solution.py:444
  68.4 0.0 copy-start.4
  68.4 0.0 copy-start.1
  68.4 3.9 %fusion.12 = f32[512,128]{1,0:T(8,128)S(1)} fusion(bf16[2,512,4608]{2,1,0:T(8,128)(2,1)} %gather_rows.1, bf16[2,4608,128]{2,1,0:T(8,128)(2,1)S(1)} %copy-done.5), kind=kOutput, calls=%fused_computation.21 | convolution fusion | flops 603979776 | bytes 6160384 | tf_op jit(solution)/shard_map/dot_general | solution.py:444
  72.3 0.5 fusion.55
  72.8 0.1 multiply_convert_fusion.1
  72.8 0.0 copy-start.2
  72.8 0.8 fusion.2
  73.6 0.8 fusion.36
  74.4 0.8 fusion.1
  75.2 2.5 %pad_maximum_fusion.part_ref = bf16[2,256,4608]{2,1,0:T(8,128)(2,1)} fusion(bf16[1,256,4608]{2,1,0:T(8,128)(2,1)S(1)} %fusion.1, bf16[1,256,4608]{2,1,0:T(8,128)(2,1)S(1)} %fusion.2), kind=kLoop, calls=%fused_computation.16 | loop fusion | flops 2359296 | bytes 9437184 | tf_op jit(solution)/shard_map/stack | solution.py:463
  77.7 82.0 %exchange.1 = (f32[2,16,4608]{2,1,0:T(8,128)}, bf16[2,256,4608]{2,1,0:T(8,128)(2,1)}) custom-call(bf16[2,256,4608]{2,1,0:T(8,128)(2,1)} %pad_maximum_fusion.part_ref, f32[2,4608]{1,0:T(2,128)} %bias_ref.1, bf16[2,16,4608]{2,1,0:T(8,128)(2,1)} %bitcast.103), custom_call_target="tpu_custom_call" | custom-call | tf_op jit(solution)/shard_map/exchange/pallas_call | solution.py:403
  159.7 2.5 %copy.14 = f32[16,2,4608]{2,1,0:T(2,128)} copy(f32[16,2,4608]{2,0,1:T(8,128)} %bitcast.104) | data formatting | bytes 1179648
  162.2 3.8 %convert_reduce_fusion = f32[2,4608]{1,0:T(2,128)} fusion(bf16[2,256,4608]{2,1,0:T(8,128)(2,1)} %get-tuple-element.8), kind=kLoop, calls=%fused_computation | loop fusion | flops 4709376 | bytes 4755456 | tf_op jit(solution)/shard_map/reduce_sum | solution.py:478
  166.0 0.8 fusion.89
  166.8 0.8 fusion.22
  167.6 0.0 slice-start.2
  167.6 0.8 fusion.88
  168.4 0.6 pad_maximum_fusion.3
  169.0 0.4 convolution_convert_fusion.6
  169.4 0.5 fusion.7
  170.0 0.8 fusion.4
  170.8 0.8 fusion.3
  171.6 0.2 pad_maximum_fusion.2
  171.9 2.4 %copy.15 = bf16[2,4608,128]{2,1,0:T(8,128)(2,1)} copy(bf16[2,4608,128]{1,2,0:T(8,128)(2,1)S(1)} %pad_maximum_fusion.2) | data formatting | bytes 4718592
  174.3 2.2 %fusion.6 = bf16[1,128,4608]{2,1,0:T(8,128)(2,1)S(1)} fusion(bf16[256,128]{1,0:T(8,128)(2,1)} %copy-done.2, bf16[2,256,4608]{2,1,0:T(8,128)(2,1)} %get-tuple-element.8), kind=kOutput, calls=%fused_computation.14 | convolution fusion | flops 302579712 | bytes 3604480 | tf_op jit(solution)/shard_map/dot_general | solution.py:475
  176.5 2.2 %fusion.5 = bf16[1,128,4608]{2,1,0:T(8,128)(2,1)S(1)} fusion(bf16[256,128]{1,0:T(8,128)(2,1)S(1)} %copy-done.3, bf16[2,256,4608]{2,1,0:T(8,128)(2,1)} %get-tuple-element.8), kind=kOutput, calls=%fused_computation.13 | convolution fusion | flops 302579712 | bytes 3604480 | tf_op jit(solution)/shard_map/dot_general | solution.py:475
  178.7 2.0 %pad_maximum_fusion.1 = bf16[3,128,4608]{2,1,0:T(8,128)(2,1)} fusion(bf16[1,128,4608]{2,1,0:T(8,128)(2,1)S(1)} %fusion.7, bf16[1,128,4608]{2,1,0:T(8,128)(2,1)S(1)} %fusion.6, bf16[1,128,4608]{2,1,0:T(8,128)(2,1)S(1)} %fusion.5), kind=kLoop, calls=%fused_computation.27 | loop fusion | flops 3538944 | bytes 7077888 | tf_op jit(solution)/shard_map/stack | solution.py:477
  (15 shorter events, 0.0 us)
Async XLA Ops:
  5.0 59.6 %copy-start.5 = (bf16[2,4608,128]{2,1,0:T(8,128)(2,1)S(1)}, bf16[2,4608,128]{2,1,0:T(8,128)(2,1)}, u32[]{:S(2)}) copy-start(bf16[2,4608,128]{2,1,0:T(8,128)(2,1)} %param.10) | copy-start | bytes 7077892
  68.4 3.9 %copy-start.4 = (s32[256]{0:T(256)S(1)}, s32[256]{0:T(256)}, u32[]{:S(2)}) copy-start(s32[256]{0:T(256)} %param.8) | copy-start | bytes 3076
  68.4 4.4 %copy-start.1 = (bf16[3,128,4608]{2,1,0:T(8,128)(2,1)S(1)}, bf16[3,128,4608]{2,1,0:T(8,128)(2,1)}, u32[]{:S(2)}) copy-start(bf16[3,128,4608]{2,1,0:T(8,128)(2,1)} %param.12) | copy-start | bytes 10616836
  72.8 0.8 copy-start.2
  159.7 6.3 %copy-start = (bf16[2,256,4608]{2,1,0:T(8,128)(2,1)S(1)}, bf16[2,256,4608]{2,1,0:T(8,128)(2,1)}, u32[]{:S(2)}) copy-start(bf16[2,256,4608]{2,1,0:T(8,128)(2,1)} %get-tuple-element.8) | copy-start | bytes 14155780
  162.2 7.8 %slice-start = ((s8[9437184]{0:T(1024)(128)(4,1)}), s8[1048576]{0:T(1024)(128)(4,1)S(1)}, s32[]{:S(2)}) async-start(s8[9437184]{0:T(1024)(128)(4,1)} %bitcast.100), calls=%async_computation | async-start | bytes 2097152
  166.0 3.9 %slice-start.1 = ((s8[9437184]{0:T(1024)(128)(4,1)}), s8[4194304]{0:T(1024)(128)(4,1)S(1)}, s32[]{:S(2)}) async-start(s8[9437184]{0:T(1024)(128)(4,1)} %bitcast.100), calls=%async_computation.1 | async-start | bytes 8388608
  167.6 2.4 %slice-start.2 = ((s8[9437184]{0:T(1024)(128)(4,1)}), s8[4194304]{0:T(1024)(128)(4,1)S(1)}, s32[]{:S(2)}) async-start(s8[9437184]{0:T(1024)(128)(4,1)} %bitcast.100), calls=%async_computation.2 | async-start | bytes 8388608
  174.3 2.2 %copy-start.3 = (bf16[256,128]{1,0:T(8,128)(2,1)S(1)}, bf16[256,128]{1,0:T(8,128)(2,1)}, u32[]{:S(2)}) copy-start(bf16[256,128]{1,0:T(8,128)(2,1)} %copy-done.2) | copy-start | bytes 196612

commit v3 on v2

--- a/solution.py
+++ b/solution.py
@@ -18,18 +18,6 @@
 
 def activate(values):
     return jax.nn.gelu(values, approximate=True)
-
-
-def recon_terms(target, latents, dec_weight, layers):
-    summed_terms = None
-    for source in range(target + 1):
-        product = jnp.dot(
-            latents[source],
-            dec_weight[pair_index(source, target, layers)],
-            preferred_element_type=jnp.float32,
-        )
-        summed_terms = product if summed_terms is None else summed_terms + product
-    return summed_terms
 
 
 def position():
@@ -208,15 +196,13 @@
         compiler_params=pltpu.CompilerParams(
             collective_id=collective_id, has_side_effects=True, vmem_limit_bytes=VMEM_LIMIT
         ),
-        name="gather_rows",
+        name=f"gather_rows_{rows}",
     )(own)
 
 
-def exchange_kernel(
-    n, factor, part_ref, bias_ref, wanted_ref, sum_ref, whole_ref,
-    own_error, core_buf, y_out, y_in, right_out, right_in, left_out, left_in,
+def scatter_kernel(
+    n, part_ref, sum_ref, core_buf, y_out, y_in, right_out, right_in, left_out, left_in,
     core_send, core_recv, y_send, y_recv, right_send, right_recv, left_send, left_recv,
-    send_sem, recv_sem, local_sem,
 ):
     long = n // 4
     layers, rows, width = sum_ref.shape
@@ -226,6 +212,9 @@
 
     def index(zz, yy, cc):
         return zz * 4 + yy * 2 + cc
+
+    def own_rows(owner):
+        return rows_of(owner, rows)
 
     def remote(src, dst, send, recv, target):
         return pltpu.make_async_remote_copy(
@@ -240,12 +229,12 @@
         if low < high:
             order.append(low)
         low, high = low + 1, high - 1
-    pieces = [(zz, t) for t in range(layers) for zz in order]
+    pieces = [(zz, t) for zz in order for t in range(layers)]
 
     def core_copy(zz, side, t):
         owner = index(zz, 1 - y if side == 0 else y, 1 - c)
         return remote(
-            part_ref.at[t, rows_of(owner, rows), :], core_buf.at[side, zz, t],
+            part_ref.at[t, own_rows(owner), :], core_buf.at[side, zz, t],
             core_send.at[side, zz, t], core_recv.at[side, zz, t], index(z, y, 1 - c),
         )
 
@@ -267,38 +256,38 @@
             index(z - 1, y, c),
         )
 
-    for zz, t in pieces:
-        for side in range(2):
+    for side in range(2):
+        for zz, t in pieces:
             core_copy(zz, side, t).start()
 
     def start_y(piece):
         zz, t = piece
         core_copy(zz, 0, t).wait_recv()
         owner = index(zz, 1 - y, c)
-        total = part_ref[t, rows_of(owner, rows), :].astype(f32) + core_buf[0, zz, t].astype(f32)
+        total = part_ref[t, own_rows(owner), :].astype(f32) + core_buf[0, zz, t].astype(f32)
         y_out[zz, t] = total.astype(y_out.dtype)
         y_copy(zz, t).start()
 
-    ahead = min(3, len(pieces))
-
-    def sum_piece(number):
-        zz, t = pieces[number]
+    ahead = 2
+    for piece in pieces[:ahead]:
+        start_y(piece)
+    for number, (zz, t) in enumerate(pieces):
         core_copy(zz, 1, t).wait_recv()
         y_copy(zz, t).wait_recv()
         if number + ahead < len(pieces):
             start_y(pieces[number + ahead])
 
-        def here():
+        def here(zz=zz, t=t):
             owner = index(zz, y, c)
             return (
-                part_ref[t, rows_of(owner, rows), :].astype(f32)
+                part_ref[t, own_rows(owner), :].astype(f32)
                 + core_buf[1, zz, t].astype(f32)
                 + y_in[zz, t].astype(f32)
             )
 
         @pl.when(zz == z)
         def _():
-            sum_ref[t] = here() + bias_ref[pl.ds(t, 1), :]
+            sum_ref[t] = here()
 
         @pl.when(zz > z)
         def _():
@@ -326,24 +315,7 @@
 
             left_copy(zz, t).start()
 
-    cuts = column_cuts(width, 2 / 3)
-    views, firsts = [], []
     for t in range(layers):
-        for cut in cuts:
-            views.append(
-                lambda owner, t=t, cut=cut: whole_ref.at[t, rows_of(owner, rows), cut]
-            )
-            firsts.append(own_error.at[t, :, cut])
-    gather = Gather(
-        long, z, y, c, views, (0, 1) * layers, firsts, send_sem, recv_sem
-    )
-
-    def local(t):
-        return pltpu.make_async_copy(
-            own_error.at[t], whole_ref.at[t, rows_of(gather.me, rows), :], local_sem.at[t]
-        )
-
-    def close(t):
         @pl.when(z > 0)
         def _():
             right_copy(z, t).wait_recv()
@@ -353,33 +325,6 @@
         def _():
             left_copy(z, t).wait_recv()
             sum_ref[t] += left_in[z, t].astype(f32)
-
-        own_error[t] = ((sum_ref[t] - wanted_ref[t].astype(f32)) * factor).astype(own_error.dtype)
-        local(t).start()
-        gather.begin(2 * t + 1)
-        gather.begin(2 * t)
-
-    def spread_step(t, step):
-        gather.line(2 * t, step)
-        if step == 1:
-            gather.across(2 * t + 1, 0)
-        gather.line(2 * t + 1, step)
-
-    for piece in pieces[:ahead]:
-        start_y(piece)
-    for t in range(layers):
-        for number in range(long):
-            sum_piece(t * long + number)
-            if t > 0 and number > 0:
-                spread_step(t - 1, number)
-        close(t)
-        if t > 0:
-            for step in range(long):
-                gather.across(2 * (t - 1), step)
-    for step in range(1, long):
-        spread_step(layers - 1, step)
-        gather.across(2 * (layers - 1), step - 1)
-    gather.across(2 * (layers - 1), long - 1)
 
     for zz, t in pieces:
         core_copy(zz, 0, t).wait_send()
@@ -387,41 +332,216 @@
         y_copy(zz, t).wait_send()
         pl.when(zz > z)(lambda zz=zz, t=t: right_copy(zz, t).wait_send())
         pl.when(zz < z)(lambda zz=zz, t=t: left_copy(zz, t).wait_send())
-    for t in range(layers):
-        gather.finish(2 * t)
-        gather.finish(2 * t + 1)
-        local(t).wait()
-
-
-def exchange(parts, bias, wanted, factor, n, collective_id):
+
+
+def scatter_sum(parts, n, collective_id):
     layers, all_rows, width = parts.shape
     rows, long = all_rows // n, n // 4
     line = pltpu.VMEM((long, layers, rows, width), parts.dtype)
     sems = pltpu.SemaphoreType.DMA((long, layers))
     two_sems = pltpu.SemaphoreType.DMA((2, long, layers))
-    vmem = pl.BlockSpec(memory_space=pltpu.VMEM)
     return pl.pallas_call(
-        functools.partial(exchange_kernel, n, factor),
-        out_shape=(
-            jax.ShapeDtypeStruct((layers, rows, width), jnp.float32),
-            jax.ShapeDtypeStruct((layers, all_rows, width), parts.dtype),
-        ),
-        in_specs=[vmem, vmem, vmem],
-        out_specs=(vmem, pl.BlockSpec(memory_space=pl.ANY)),
+        functools.partial(scatter_kernel, n),
+        out_shape=jax.ShapeDtypeStruct((layers, rows, width), jnp.float32),
+        in_specs=[pl.BlockSpec(memory_space=pltpu.VMEM)],
+        out_specs=pl.BlockSpec(memory_space=pltpu.VMEM),
         scratch_shapes=[
-            pltpu.VMEM((layers, rows, width), parts.dtype),
             pltpu.VMEM((2, long, layers, rows, width), parts.dtype),
             line, line, line, line, line, line,
             two_sems, two_sems, sems, sems, sems, sems, sems, sems,
-            pltpu.SemaphoreType.DMA((2 * layers, 4, n)),
-            pltpu.SemaphoreType.DMA((2 * layers, n)),
-            pltpu.SemaphoreType.DMA((layers,)),
         ],
         compiler_params=pltpu.CompilerParams(
             collective_id=collective_id, has_side_effects=True, vmem_limit_bytes=VMEM_LIMIT
         ),
-        name="exchange",
-    )(parts, bias, wanted)
+        name="scatter_sum",
+    )(parts)
+
+
+def front_kernel(
+    tiles, slot_ref, slots_ref, enc_ref, ebias_ref, dec_ref, pre_ref, latent_ref, part_ref, total
+):
+    step = pl.program_id(0)
+    f32, bf16 = jnp.float32, jnp.bfloat16
+    layers, slot_count, _ = slots_ref.shape
+
+    @pl.when(step == 0)
+    def _():
+        total[...] = jnp.zeros_like(total)
+
+    @pl.when(step < tiles)
+    def _():
+        for source in range(layers):
+            total[source] += jnp.dot(
+                slots_ref[source], enc_ref[source], preferred_element_type=f32
+            )
+
+    @pl.when(step == tiles - 1)
+    def _():
+        shape = (slot_ref.shape[0], slot_count)
+        pick = (slot_ref[...] == lax.broadcasted_iota(jnp.int32, shape, 1)).astype(f32)
+        pick = pick.astype(bf16)
+        for source in range(layers):
+            rest = total[source]
+            row_pre = None
+            for _ in range(3):
+                term = rest.astype(bf16)
+                rest = rest - term.astype(f32)
+                product = jnp.dot(pick, term, preferred_element_type=f32)
+                row_pre = product if row_pre is None else row_pre + product
+            pre_acts = row_pre + ebias_ref[pl.ds(source, 1), :]
+            pre_ref[source] = pre_acts
+            latent_ref[source] = activate(pre_acts).astype(bf16)
+
+    @pl.when(step >= tiles)
+    def _():
+        for target in range(layers):
+            summed = None
+            for source in range(target + 1):
+                product = jnp.dot(
+                    latent_ref[source],
+                    dec_ref[pair_index(source, target, layers)],
+                    preferred_element_type=f32,
+                )
+                summed = product if summed is None else summed + product
+            part_ref[target] = summed.astype(part_ref.dtype)
+
+
+def tile_of(width):
+    return 512 if width % 512 == 0 else width
+
+
+def front(row_slot, slots, enc_weight, enc_bias, dec_weight, part_dtype):
+    layers, slot_count, width = slots.shape
+    pairs, wide, _ = dec_weight.shape
+    row_count = row_slot.shape[0]
+    tile = tile_of(width)
+    tiles = width // tile
+
+    def early(step):
+        return jnp.minimum(step, tiles - 1)
+
+    def late(step):
+        return jnp.maximum(step - tiles, 0)
+
+    return pl.pallas_call(
+        functools.partial(front_kernel, tiles),
+        grid=(2 * tiles,),
+        out_shape=(
+            jax.ShapeDtypeStruct((layers, row_count, wide), jnp.float32),
+            jax.ShapeDtypeStruct((layers, row_count, wide), jnp.bfloat16),
+            jax.ShapeDtypeStruct((layers, row_count, width), part_dtype),
+        ),
+        in_specs=[
+            pl.BlockSpec((row_count, 1), lambda i: (0, 0)),
+            pl.BlockSpec((layers, slot_count, tile), lambda i: (0, 0, early(i))),
+            pl.BlockSpec((layers, tile, wide), lambda i: (0, early(i), 0)),
+            pl.BlockSpec((layers, wide), lambda i: (0, 0)),
+            pl.BlockSpec((pairs, wide, tile), lambda i: (0, 0, late(i))),
+        ],
+        out_specs=(
+            pl.BlockSpec((layers, row_count, wide), lambda i: (0, 0, 0)),
+            pl.BlockSpec((layers, row_count, wide), lambda i: (0, 0, 0)),
+            pl.BlockSpec((layers, row_count, tile), lambda i: (0, 0, late(i))),
+        ),
+        scratch_shapes=[pltpu.VMEM((layers, slot_count, wide), jnp.float32)],
+        compiler_params=pltpu.CompilerParams(vmem_limit_bytes=VMEM_LIMIT),
+        name="front",
+    )(row_slot[:, None], slots, enc_weight, enc_bias, dec_weight)
+
+
+def tail_kernel(
+    tiles, slot_ref, pre_ref, latent_ref, errors_ref, dec_ref, slots_ref,
+    gdec_ref, gdbias_ref, gebias_ref, genc_ref, back, spread,
+):
+    step = pl.program_id(0)
+    f32, bf16 = jnp.float32, jnp.bfloat16
+    layers, slot_count, _ = slots_ref.shape
+    over_rows = (((0,), (0,)), ((), ()))
+    over_width = (((1,), (1,)), ((), ()))
+
+    @pl.when(step == 0)
+    def _():
+        back[...] = jnp.zeros_like(back)
+
+    @pl.when(step < tiles)
+    def _():
+        for target in range(layers):
+            error = errors_ref[target]
+            gdbias_ref[pl.ds(target, 1), :] = jnp.sum(error.astype(f32), axis=0, keepdims=True)
+            for source in range(target + 1):
+                pair = pair_index(source, target, layers)
+                gdec_ref[pair] = lax.dot_general(
+                    latent_ref[source], error, over_rows, preferred_element_type=f32
+                ).astype(gdec_ref.dtype)
+                back[source] += lax.dot_general(
+                    error, dec_ref[pair], over_width, preferred_element_type=f32
+                )
+
+    @pl.when(step == tiles - 1)
+    def _():
+        shape = (slot_count, slot_ref.shape[1])
+        place = (slot_ref[...] == lax.broadcasted_iota(jnp.int32, shape, 0)).astype(f32)
+        place = place.astype(bf16)
+        for source in range(layers):
+            unused, pullback = jax.vjp(activate, pre_ref[source])
+            dpre = pullback(back[source])[0]
+            gebias_ref[pl.ds(source, 1), :] = jnp.sum(dpre, axis=0, keepdims=True)
+            spread[source] = jnp.dot(
+                place, dpre.astype(bf16), preferred_element_type=f32
+            ).astype(bf16)
+
+    @pl.when(step >= tiles)
+    def _():
+        for source in range(layers):
+            genc_ref[source] = lax.dot_general(
+                slots_ref[source], spread[source], over_rows, preferred_element_type=f32
+            ).astype(genc_ref.dtype)
+
+
+def tail(row_slot, pre, latents, errors, dec_weight, slots):
+    layers, slot_count, width = slots.shape
+    pairs, wide, _ = dec_weight.shape
+    row_count = row_slot.shape[0]
+    tile = tile_of(width)
+    tiles = width // tile
+    bf16 = jnp.bfloat16
+
+    def early(step):
+        return jnp.minimum(step, tiles - 1)
+
+    def late(step):
+        return jnp.maximum(step - tiles, 0)
+
+    return pl.pallas_call(
+        functools.partial(tail_kernel, tiles),
+        grid=(2 * tiles,),
+        out_shape=(
+            jax.ShapeDtypeStruct((pairs, wide, width), bf16),
+            jax.ShapeDtypeStruct((layers, width), jnp.float32),
+            jax.ShapeDtypeStruct((layers, wide), jnp.float32),
+            jax.ShapeDtypeStruct((layers, width, wide), bf16),
+        ),
+        in_specs=[
+            pl.BlockSpec((1, row_count), lambda i: (0, 0)),
+            pl.BlockSpec((layers, row_count, wide), lambda i: (0, 0, 0)),
+            pl.BlockSpec((layers, row_count, wide), lambda i: (0, 0, 0)),
+            pl.BlockSpec((layers, row_count, tile), lambda i: (0, 0, early(i))),
+            pl.BlockSpec((pairs, wide, tile), lambda i: (0, 0, early(i))),
+            pl.BlockSpec((layers, slot_count, tile), lambda i: (0, 0, late(i))),
+        ],
+        out_specs=(
+            pl.BlockSpec((pairs, wide, tile), lambda i: (0, 0, early(i))),
+            pl.BlockSpec((layers, tile), lambda i: (0, early(i))),
+            pl.BlockSpec((layers, wide), lambda i: (0, 0)),
+            pl.BlockSpec((layers, tile, wide), lambda i: (0, late(i), 0)),
+        ),
+        scratch_shapes=[
+            pltpu.VMEM((layers, row_count, wide), jnp.float32),
+            pltpu.VMEM((layers, slot_count, wide), bf16),
+        ],
+        compiler_params=pltpu.CompilerParams(vmem_limit_bytes=VMEM_LIMIT),
+        name="tail",
+    )(row_slot[None, :], pre, latents, errors, dec_weight, slots)
 
 
 def plain_gather(own):
@@ -437,80 +557,21 @@
 
     store = jnp.transpose(row_store, (1, 0, 2))
     slots = gather_rows(store, n, 0) if by_kernel else plain_gather(store)
-    slot_count = slots.shape[1]
-    pick = row_slot[:, None] == jnp.arange(slot_count, dtype=row_slot.dtype)[None, :]
-    slot_pre = jnp.concatenate(
-        [
-            jnp.dot(slots[source], enc_weight[source], preferred_element_type=f32)
-            for source in range(layers)
-        ],
-        axis=1,
+    pre, latents, parts = front(
+        row_slot, slots, enc_weight, enc_bias, dec_weight, bf16 if by_kernel else f32
     )
-    row_pre = jnp.dot(
-        pick.astype(f32), slot_pre, precision=lax.Precision.HIGHEST, preferred_element_type=f32
+    if by_kernel:
+        summed = scatter_sum(parts, n, 1)
+    else:
+        summed = lax.psum_scatter(parts, "latent", scatter_dimension=1, tiled=True)
+    rebuilt = summed + dec_bias[:, None, :]
+    factor = 1.0 / math.sqrt(row_count)
+    wanted = jnp.transpose(targets, (1, 0, 2)).astype(f32)
+    error_part = ((rebuilt - wanted) * factor).astype(bf16)
+    errors = gather_rows(error_part, n, 2) if by_kernel else plain_gather(error_part)
+    grad_dec, grad_dbias, grad_ebias, grad_enc = tail(
+        row_slot, pre, latents, errors, dec_weight, slots
     )
-    wide = enc_weight.shape[2]
-    pre_list = []
-    latents = []
-    for source in range(layers):
-        pre_acts = row_pre[:, source * wide : (source + 1) * wide] + enc_bias[source][None, :]
-        pre_list.append(pre_acts)
-        latents.append(activate(pre_acts).astype(bf16))
-    terms = [recon_terms(target, latents, dec_weight, layers) for target in range(layers)]
-    factor = 1.0 / math.sqrt(row_count)
-    wanted = jnp.transpose(targets, (1, 0, 2))
-    if by_kernel:
-        parts = jnp.stack([term.astype(bf16) for term in terms], axis=0)
-        rebuilt, errors = exchange(parts, dec_bias, wanted, factor, n, 1)
-    else:
-        summed = lax.psum_scatter(
-            jnp.stack(terms, axis=0), "latent", scatter_dimension=1, tiled=True
-        )
-        rebuilt = summed + dec_bias[:, None, :]
-        errors = plain_gather(((rebuilt - wanted.astype(f32)) * factor).astype(bf16))
-    grad_dec_list = []
-    for source in range(layers):
-        for target in range(source, layers):
-            grad_dec_list.append(
-                jnp.dot(latents[source].T, errors[target], preferred_element_type=f32).astype(bf16)
-            )
-    grad_dec = jnp.stack(grad_dec_list, axis=0)
-    grad_dbias = jnp.sum(errors.astype(f32), axis=1)
-    grad_ebias_list = []
-    low_list = []
-    for source in range(layers):
-        back = None
-        for target in range(source, layers):
-            product = lax.dot_general(
-                errors[target],
-                dec_weight[pair_index(source, target, layers)],
-                (((1,), (1,)), ((), ())),
-                preferred_element_type=f32,
-            )
-            back = product if back is None else back + product
-        unused, pullback = jax.vjp(activate, pre_list[source])
-        dpre = pullback(back)[0]
-        grad_ebias_list.append(jnp.sum(dpre, axis=0))
-        low_list.append(dpre.astype(bf16))
-    slot_dpre = lax.dot_general(
-        pick.astype(bf16),
-        jnp.concatenate(low_list, axis=1),
-        (((0,), (0,)), ((), ())),
-        preferred_element_type=f32,
-    ).astype(bf16)
-    grad_enc = jnp.stack(
-        [
-            lax.dot_general(
-                slots[source],
-                slot_dpre[:, source * wide : (source + 1) * wide],
-                (((0,), (0,)), ((), ())),
-                preferred_element_type=f32,
-            ).astype(bf16)
-            for source in range(layers)
-        ],
-        axis=0,
-    )
-    grad_ebias = jnp.stack(grad_ebias_list, axis=0)
     return (jnp.transpose(rebuilt, (1, 0, 2)), grad_enc, grad_ebias, grad_dec, grad_dbias)
 
 

time: 181 us -> 181 us (level)
  Pallas kernels: 142 us -> 173 us
  matrix products: 19.7 us -> 0 us
  other arithmetic: 9.24 us -> 1.87 us
  local copies, waits for them, and re-layouts: 9.36 us -> 4.69 us
    pallas_call x1 -> x2, Pallas kernels: 59.6 us -> 99 us  [gather_rows(): pl.pallas_call(functools.partial(gather_kernel, n), out_shape=jax.ShapeDt...]
    dot_general x15 -> x0, matrix products: 19.7 us -> none  [the longest x2 7.57 us: body(): jnp.dot(slots[source], enc_weight[source], preferred_element_type=f32)]
    pallas_call x1 -> x3, Pallas kernels: 82 us -> 73.8 us  [the longest x1 37 us: scatter_sum(): pl.pallas_call(functools.partial(scatter_kernel, n), out_shape=jax.ShapeD...]
    unnamed x22 -> x6, local copies, waits for them, and re-layouts: 8.6 us -> 3.21 us
    another operation x4 -> x0, other arithmetic: 5.34 us -> none  [the longest x1 2.54 us: body(): parts = jnp.stack([term.astype(bf16) for term in terms], axis=0)]
    reduce_sum x1 -> x0, other arithmetic: 3.85 us -> none  [body(): grad_dbias = jnp.sum(errors.astype(f32), axis=1)]
where the time goes in v3:
time: 181 us; the launch traced here: 180 us
  Pallas kernels  173 us (96%)
  local copies, waits for them, and re-layouts  4.69 us (3%)
  other arithmetic  1.87 us (1%)
    pallas_call x2, Pallas kernels, gather_rows(): pl.pallas_call(functools.partial(gather_kernel, n), out_shape=jax.ShapeDt...  99 us
    pallas_call x1, Pallas kernels, scatter_sum(): pl.pallas_call(functools.partial(scatter_kernel, n), out_shape=jax.ShapeD...  37 us
    pallas_call x1, Pallas kernels, tail(): pl.pallas_call(functools.partial(tail_kernel, tiles), grid=(2 * tiles,),...  19.3 us
    pallas_call x1, Pallas kernels, front(): pl.pallas_call(functools.partial(front_kernel, tiles), grid=(2 * tiles,),...  17.5 us

profile of v3, /device:TPU:0, one launch (start us, length us, event | category | flops | bytes accessed | tf_op | source)
XLA Modules:
  0.0 180.0 jit_solution(13689501692986237446)
XLA Ops:
  0.6 1.5 copy.16.slot_ref
  2.1 1.9 %copy.21 = bf16[32,2,4608]{2,0,1:T(8,128)(2,1)} copy(bf16[32,2,4608]{2,1,0:T(2,128)(2,1)} %param.7) | data formatting | bytes 1179648 | tf_op args[0]
  4.0 59.6 %gather_rows_32.1.slots_ref = bf16[2,512,4608]{2,1,0:T(8,128)(2,1)} custom-call(bf16[2,32,4608]{2,1,0:T(8,128)(2,1)} %bitcast.13), custom_call_target="tpu_custom_call" | custom-call | tf_op jit(solution)/shard_map/gather_rows_32/pallas_call | solution.py:186
  63.7 17.5 %front.1 = (f32[2,256,128]{2,1,0:T(8,128)}, bf16[2,256,128]{2,1,0:T(8,128)(2,1)}, bf16[2,256,4608]{2,1,0:T(8,128)(2,1)}) custom-call(s32[256,1]{1,0:T(8,128)} %copy.16.slot_ref, bf16[2,512,4608]{2,1,0:T(8,128)(2,1)} %gather_rows_32.1.slots_ref, bf16[2,4608,128]{2,1,0:T(8,128)(2,1)} %enc_ref.1, f32[2,128]{1,0:T(2,128)} %ebias_ref.1, bf16[3,128,4608]{2,1,0:T(8,128)(2,1)} %dec_ref.3), custom_call_target="tpu_custom_call" | custom-call | tf_op jit(solution)/shard_map/front/pallas_call | solution.py:426
  81.2 0.0 copy-start
  81.2 0.0 copy-start.1
  81.2 37.0 %scatter_sum.1 = f32[2,16,4608]{2,1,0:T(8,128)} custom-call(bf16[2,256,4608]{2,1,0:T(8,128)(2,1)} %get-tuple-element.12.part_ref), custom_call_target="tpu_custom_call" | custom-call | tf_op jit(solution)/shard_map/scatter_sum/pallas_call | solution.py:343
  118.2 0.0 copy-done
  118.2 0.0 copy-done.1
  118.2 1.9 %fusion.1 = (bf16[2,16,4608]{2,1,0:T(8,128)(2,1)}, f32[16,2,4608]{2,0,1:T(8,128)S(1)}) fusion(f32[2,16,4608]{2,1,0:T(8,128)} %scatter_sum.1, bf16[16,2,4608]{2,1,0:T(2,128)(2,1)S(1)} %copy-done, f32[2,4608]{1,0:T(2,128)S(1)} %copy-done.1), kind=kLoop, calls=%fused_computation.2 | loop fusion | flops 737280 | bytes 1806336 | tf_op jit(solution)/shard_map/convert_element_type | solution.py:570
  120.1 1.3 copy.18
  121.4 39.4 %gather_rows_16.1.errors_ref = bf16[2,256,4608]{2,1,0:T(8,128)(2,1)} custom-call(bf16[2,16,4608]{2,1,0:T(8,128)(2,1)} %get-tuple-element.29.own_ref), custom_call_target="tpu_custom_call" | custom-call | tf_op jit(solution)/shard_map/gather_rows_16/pallas_call | solution.py:186
  160.7 19.3 %tail.1 = (bf16[3,128,4608]{2,1,0:T(8,128)(2,1)}, f32[2,4608]{1,0:T(2,128)}, f32[2,128]{1,0:T(2,128)}, bf16[2,4608,128]{2,1,0:T(8,128)(2,1)}) custom-call(s32[1,256]{1,0:T(1,128)} %bitcast.15, f32[2,256,128]{2,1,0:T(8,128)} %get-tuple-element.13.pre_ref, bf16[2,256,128]{2,1,0:T(8,128)(2,1)} %get-tuple-element.14.latent_ref, ...), custom_call_target="tpu_custom_call" | custom-call | tf_op jit(solution)/shard_map/tail/pallas_call | solution.py:515
Async XLA Ops:
  81.2 37.0 %copy-start = (bf16[16,2,4608]{2,1,0:T(2,128)(2,1)S(1)}, bf16[16,2,4608]{2,1,0:T(2,128)(2,1)}, u32[]{:S(2)}) copy-start(bf16[16,2,4608]{2,1,0:T(2,128)(2,1)} %param.9) | copy-start | bytes 884740
  81.2 37.0 %copy-start.1 = (f32[2,4608]{1,0:T(2,128)S(1)}, f32[2,4608]{1,0:T(2,128)}, u32[]{:S(2)}) copy-start(f32[2,4608]{1,0:T(2,128)} %param.13) | copy-start | bytes 110596

commit v4 on v2

--- a/solution.py
+++ b/solution.py
@@ -156,67 +156,71 @@
             self.copy(part, 2, self.me).wait_send()
 
 
-def column_cuts(width, share):
-    cut = int(width * share) // 128 * 128
-    return (pl.ds(0, cut), pl.ds(cut, width - cut))
-
-
 def rows_of(owner, rows):
     return pl.ds(pl.multiple_of(owner * rows, rows), rows)
 
 
-def gather_kernel(n, own_ref, whole_ref, send_sem, recv_sem, local_sem):
+def gather_kernel(n, share, own_ref, whole_ref, send_sem, recv_sem, local_sem):
     long = n // 4
     layers, rows, width = own_ref.shape
     z, y, c = position()
     greet(long, z, y, c)
-    cuts = column_cuts(width, 5 / 6)
-    views = [
-        lambda owner, cut=cut: whole_ref.at[:, rows_of(owner, rows), cut] for cut in cuts
-    ]
-    firsts = [own_ref.at[:, :, cut] for cut in cuts]
-    gather = Gather(long, z, y, c, views, (0, 1), firsts, send_sem, recv_sem)
+    cut = int(width * share) // 128 * 128
+    cuts = [pl.ds(0, cut)] if cut == width else [pl.ds(0, cut), pl.ds(cut, width - cut)]
+    views, firsts, routes = [], [], []
+    for t in range(layers):
+        for route, columns in enumerate(cuts):
+            views.append(
+                lambda owner, t=t, columns=columns: whole_ref.at[t, rows_of(owner, rows), columns]
+            )
+            firsts.append(own_ref.at[t, :, columns])
+            routes.append(route)
+    gather = Gather(long, z, y, c, views, routes, firsts, send_sem, recv_sem)
     local = pltpu.make_async_copy(
         own_ref, whole_ref.at[:, rows_of(gather.me, rows), :], local_sem
     )
     local.start()
-    gather.begin(1)
-    gather.begin(0)
-    gather.across(1, 0)
+    straight = [part for part, route in enumerate(routes) if route == 0]
+    turned = [part for part, route in enumerate(routes) if route == 1]
+    for part in turned + straight:
+        gather.begin(part)
+    for part in turned:
+        gather.across(part, 0)
     for step in range(1, long):
-        gather.line(0, step)
-        gather.line(1, step)
-        gather.across(0, step - 1)
-    gather.across(0, long - 1)
-    gather.finish(0)
-    gather.finish(1)
+        for part in straight + turned:
+            gather.line(part, step)
+        for part in straight:
+            gather.across(part, step - 1)
+    for part in straight:
+        gather.across(part, long - 1)
+    for part in straight + turned:
+        gather.finish(part)
     local.wait()
 
 
-def gather_rows(own, n, collective_id):
+def gather_rows(own, n, share, collective_id):
     layers, rows, width = own.shape
+    parts = layers if share == 1 else 2 * layers
     return pl.pallas_call(
-        functools.partial(gather_kernel, n),
+        functools.partial(gather_kernel, n, share),
         out_shape=jax.ShapeDtypeStruct((layers, n * rows, width), own.dtype),
         in_specs=[pl.BlockSpec(memory_space=pl.ANY)],
         out_specs=pl.BlockSpec(memory_space=pl.ANY),
         scratch_shapes=[
-            pltpu.SemaphoreType.DMA((2, 4, n)),
-            pltpu.SemaphoreType.DMA((2, n)),
+            pltpu.SemaphoreType.DMA((parts, 4, n)),
+            pltpu.SemaphoreType.DMA((parts, n)),
             pltpu.SemaphoreType.DMA,
         ],
         compiler_params=pltpu.CompilerParams(
             collective_id=collective_id, has_side_effects=True, vmem_limit_bytes=VMEM_LIMIT
         ),
-        name="gather_rows",
+        name=f"gather_rows_{rows}",
     )(own)
 
 
-def exchange_kernel(
-    n, factor, part_ref, bias_ref, wanted_ref, sum_ref, whole_ref,
-    own_error, core_buf, y_out, y_in, right_out, right_in, left_out, left_in,
+def scatter_kernel(
+    n, part_ref, sum_ref, core_buf, y_out, y_in, right_out, right_in, left_out, left_in,
     core_send, core_recv, y_send, y_recv, right_send, right_recv, left_send, left_recv,
-    send_sem, recv_sem, local_sem,
 ):
     long = n // 4
     layers, rows, width = sum_ref.shape
@@ -226,6 +230,9 @@
 
     def index(zz, yy, cc):
         return zz * 4 + yy * 2 + cc
+
+    def own_rows(owner):
+        return rows_of(owner, rows)
 
     def remote(src, dst, send, recv, target):
         return pltpu.make_async_remote_copy(
@@ -240,12 +247,12 @@
         if low < high:
             order.append(low)
         low, high = low + 1, high - 1
-    pieces = [(zz, t) for t in range(layers) for zz in order]
+    pieces = [(zz, t) for zz in order for t in range(layers)]
 
     def core_copy(zz, side, t):
         owner = index(zz, 1 - y if side == 0 else y, 1 - c)
         return remote(
-            part_ref.at[t, rows_of(owner, rows), :], core_buf.at[side, zz, t],
+            part_ref.at[t, own_rows(owner), :], core_buf.at[side, zz, t],
             core_send.at[side, zz, t], core_recv.at[side, zz, t], index(z, y, 1 - c),
         )
 
@@ -267,38 +274,38 @@
             index(z - 1, y, c),
         )
 
-    for zz, t in pieces:
-        for side in range(2):
+    for side in range(2):
+        for zz, t in pieces:
             core_copy(zz, side, t).start()
 
     def start_y(piece):
         zz, t = piece
         core_copy(zz, 0, t).wait_recv()
         owner = index(zz, 1 - y, c)
-        total = part_ref[t, rows_of(owner, rows), :].astype(f32) + core_buf[0, zz, t].astype(f32)
+        total = part_ref[t, own_rows(owner), :].astype(f32) + core_buf[0, zz, t].astype(f32)
         y_out[zz, t] = total.astype(y_out.dtype)
         y_copy(zz, t).start()
 
-    ahead = min(3, len(pieces))
-
-    def sum_piece(number):
-        zz, t = pieces[number]
+    ahead = 2
+    for piece in pieces[:ahead]:
+        start_y(piece)
+    for number, (zz, t) in enumerate(pieces):
         core_copy(zz, 1, t).wait_recv()
         y_copy(zz, t).wait_recv()
         if number + ahead < len(pieces):
             start_y(pieces[number + ahead])
 
-        def here():
+        def here(zz=zz, t=t):
             owner = index(zz, y, c)
             return (
-                part_ref[t, rows_of(owner, rows), :].astype(f32)
+                part_ref[t, own_rows(owner), :].astype(f32)
                 + core_buf[1, zz, t].astype(f32)
                 + y_in[zz, t].astype(f32)
             )
 
         @pl.when(zz == z)
         def _():
-            sum_ref[t] = here() + bias_ref[pl.ds(t, 1), :]
+            sum_ref[t] = here()
 
         @pl.when(zz > z)
         def _():
@@ -326,24 +333,7 @@
 
             left_copy(zz, t).start()
 
-    cuts = column_cuts(width, 2 / 3)
-    views, firsts = [], []
     for t in range(layers):
-        for cut in cuts:
-            views.append(
-                lambda owner, t=t, cut=cut: whole_ref.at[t, rows_of(owner, rows), cut]
-            )
-            firsts.append(own_error.at[t, :, cut])
-    gather = Gather(
-        long, z, y, c, views, (0, 1) * layers, firsts, send_sem, recv_sem
-    )
-
-    def local(t):
-        return pltpu.make_async_copy(
-            own_error.at[t], whole_ref.at[t, rows_of(gather.me, rows), :], local_sem.at[t]
-        )
-
-    def close(t):
         @pl.when(z > 0)
         def _():
             right_copy(z, t).wait_recv()
@@ -353,33 +343,6 @@
         def _():
             left_copy(z, t).wait_recv()
             sum_ref[t] += left_in[z, t].astype(f32)
-
-        own_error[t] = ((sum_ref[t] - wanted_ref[t].astype(f32)) * factor).astype(own_error.dtype)
-        local(t).start()
-        gather.begin(2 * t + 1)
-        gather.begin(2 * t)
-
-    def spread_step(t, step):
-        gather.line(2 * t, step)
-        if step == 1:
-            gather.across(2 * t + 1, 0)
-        gather.line(2 * t + 1, step)
-
-    for piece in pieces[:ahead]:
-        start_y(piece)
-    for t in range(layers):
-        for number in range(long):
-            sum_piece(t * long + number)
-            if t > 0 and number > 0:
-                spread_step(t - 1, number)
-        close(t)
-        if t > 0:
-            for step in range(long):
-                gather.across(2 * (t - 1), step)
-    for step in range(1, long):
-        spread_step(layers - 1, step)
-        gather.across(2 * (layers - 1), step - 1)
-    gather.across(2 * (layers - 1), long - 1)
 
     for zz, t in pieces:
         core_copy(zz, 0, t).wait_send()
@@ -387,41 +350,29 @@
         y_copy(zz, t).wait_send()
         pl.when(zz > z)(lambda zz=zz, t=t: right_copy(zz, t).wait_send())
         pl.when(zz < z)(lambda zz=zz, t=t: left_copy(zz, t).wait_send())
-    for t in range(layers):
-        gather.finish(2 * t)
-        gather.finish(2 * t + 1)
-        local(t).wait()
-
-
-def exchange(parts, bias, wanted, factor, n, collective_id):
+
+
+def scatter_sum(parts, n, collective_id):
     layers, all_rows, width = parts.shape
     rows, long = all_rows // n, n // 4
     line = pltpu.VMEM((long, layers, rows, width), parts.dtype)
     sems = pltpu.SemaphoreType.DMA((long, layers))
     two_sems = pltpu.SemaphoreType.DMA((2, long, layers))
-    vmem = pl.BlockSpec(memory_space=pltpu.VMEM)
     return pl.pallas_call(
-        functools.partial(exchange_kernel, n, factor),
-        out_shape=(
-            jax.ShapeDtypeStruct((layers, rows, width), jnp.float32),
-            jax.ShapeDtypeStruct((layers, all_rows, width), parts.dtype),
-        ),
-        in_specs=[vmem, vmem, vmem],
-        out_specs=(vmem, pl.BlockSpec(memory_space=pl.ANY)),
+        functools.partial(scatter_kernel, n),
+        out_shape=jax.ShapeDtypeStruct((layers, rows, width), jnp.float32),
+        in_specs=[pl.BlockSpec(memory_space=pltpu.VMEM)],
+        out_specs=pl.BlockSpec(memory_space=pltpu.VMEM),
         scratch_shapes=[
-            pltpu.VMEM((layers, rows, width), parts.dtype),
             pltpu.VMEM((2, long, layers, rows, width), parts.dtype),
             line, line, line, line, line, line,
             two_sems, two_sems, sems, sems, sems, sems, sems, sems,
-            pltpu.SemaphoreType.DMA((2 * layers, 4, n)),
-            pltpu.SemaphoreType.DMA((2 * layers, n)),
-            pltpu.SemaphoreType.DMA((layers,)),
         ],
         compiler_params=pltpu.CompilerParams(
             collective_id=collective_id, has_side_effects=True, vmem_limit_bytes=VMEM_LIMIT
         ),
-        name="exchange",
-    )(parts, bias, wanted)
+        name="scatter_sum",
+    )(parts)
 
 
 def plain_gather(own):
@@ -436,7 +387,7 @@
     by_kernel = n % 4 == 0 and row_store.shape[0] % 16 == 0 and own_rows % 16 == 0
 
     store = jnp.transpose(row_store, (1, 0, 2))
-    slots = gather_rows(store, n, 0) if by_kernel else plain_gather(store)
+    slots = gather_rows(store, n, 5 / 6, 0) if by_kernel else plain_gather(store)
     slot_count = slots.shape[1]
     pick = row_slot[:, None] == jnp.arange(slot_count, dtype=row_slot.dtype)[None, :]
     slot_pre = jnp.concatenate(
@@ -457,17 +408,17 @@
         pre_list.append(pre_acts)
         latents.append(activate(pre_acts).astype(bf16))
     terms = [recon_terms(target, latents, dec_weight, layers) for target in range(layers)]
-    factor = 1.0 / math.sqrt(row_count)
-    wanted = jnp.transpose(targets, (1, 0, 2))
     if by_kernel:
-        parts = jnp.stack([term.astype(bf16) for term in terms], axis=0)
-        rebuilt, errors = exchange(parts, dec_bias, wanted, factor, n, 1)
+        summed = scatter_sum(jnp.stack([term.astype(bf16) for term in terms], axis=0), n, 1)
     else:
         summed = lax.psum_scatter(
             jnp.stack(terms, axis=0), "latent", scatter_dimension=1, tiled=True
         )
-        rebuilt = summed + dec_bias[:, None, :]
-        errors = plain_gather(((rebuilt - wanted.astype(f32)) * factor).astype(bf16))
+    rebuilt = summed + dec_bias[:, None, :]
+    factor = 1.0 / math.sqrt(row_count)
+    wanted = jnp.transpose(targets, (1, 0, 2)).astype(f32)
+    error_part = ((rebuilt - wanted) * factor).astype(bf16)
+    errors = gather_rows(error_part, n, 1, 2) if by_kernel else plain_gather(error_part)
     grad_dec_list = []
     for source in range(layers):
         for target in range(source, layers):

time: 181 us -> 169 us (0.934)
  Pallas kernels: 142 us -> 130 us
  local copies, waits for them, and re-layouts: 9.36 us -> 6.45 us
  other arithmetic: 9.24 us -> 11.3 us
    pallas_call x2 -> x3, Pallas kernels: 142 us -> 130 us  [the longest x2 93.4 us: gather_rows(): pl.pallas_call(functools.partial(gather_kernel, n, share), out_shape=jax....]
    unnamed x22 -> x25, local copies, waits for them, and re-layouts: 8.6 us -> 5.69 us
    convert_element_type x0 -> x1, other arithmetic: none -> 1.87 us  [body(): error_part = ((rebuilt - wanted) * factor).astype(bf16)]
where the time goes in v4:
time: 169 us
  Pallas kernels  130 us (77%)
  matrix products  19.7 us (12%)
  other arithmetic  11.3 us (7%)
  local copies, waits for them, and re-layouts  6.45 us (4%)
    pallas_call x2, Pallas kernels, gather_rows(): pl.pallas_call(functools.partial(gather_kernel, n, share), out_shape=jax....  93.4 us
    pallas_call x1, Pallas kernels, scatter_sum(): pl.pallas_call(functools.partial(scatter_kernel, n), out_shape=jax.ShapeD...  37 us
    dot_general x2, matrix products, body(): jnp.dot(slots[source], enc_weight[source], preferred_element_type=f32)  7.57 us
    unnamed x25, local copies, waits for them, and re-layouts  5.69 us
    dot_general x3, matrix products, body(): jnp.dot(latents[source].T, errors[target], preferred_element_type=f32)  4.93 us
    reduce_sum x1, other arithmetic, body(): grad_dbias = jnp.sum(errors.astype(f32), axis=1)  3.91 us

profile of v4, /device:TPU:0, one launch (start us, length us, event | category | flops | bytes accessed | tf_op | source)
XLA Modules:
  0.0 168.7 jit_solution(12461085016294736491)
XLA Ops:
  0.6 0.8 slice_bitcast_fusion
  1.4 1.9 %copy.18 = bf16[32,2,4608]{2,0,1:T(8,128)(2,1)} copy(bf16[32,2,4608]{2,1,0:T(2,128)(2,1)} %param.7) | data formatting | bytes 1179648 | tf_op args[0]
  3.3 57.0 %gather_rows_32.1 = bf16[2,512,4608]{2,1,0:T(8,128)(2,1)} custom-call(bf16[2,32,4608]{2,1,0:T(8,128)(2,1)} %bitcast.106), custom_call_target="tpu_custom_call" | custom-call | tf_op jit(solution)/shard_map/gather_rows_32/pallas_call | solution.py:204
  60.3 3.7 %fusion.9 = f32[512,128]{1,0:T(8,128)S(1)} fusion(bf16[2,512,4608]{2,1,0:T(8,128)(2,1)} %gather_rows_32.1, bf16[2,4608,128]{2,1,0:T(8,128)(2,1)S(1)} %copy-done.7), kind=kOutput, calls=%fused_computation.18 | convolution fusion | flops 603979776 | bytes 6160384 | tf_op jit(solution)/shard_map/dot_general | solution.py:395
  64.1 0.0 copy-start.6
  64.1 0.0 copy-start.1
  64.1 3.9 %fusion.12 = f32[512,128]{1,0:T(8,128)S(1)} fusion(bf16[2,512,4608]{2,1,0:T(8,128)(2,1)} %gather_rows_32.1, bf16[2,4608,128]{2,1,0:T(8,128)(2,1)S(1)} %copy-done.7), kind=kOutput, calls=%fused_computation.21 | convolution fusion | flops 603979776 | bytes 6160384 | tf_op jit(solution)/shard_map/dot_general | solution.py:395
  68.0 0.5 fusion.57
  68.4 0.1 multiply_convert_fusion.1
  68.5 0.0 copy-start.2
  68.5 0.8 fusion.2
  69.3 0.8 fusion.36
  70.1 0.8 fusion.1
  70.9 2.6 %pad_maximum_fusion.part_ref = bf16[2,256,4608]{2,1,0:T(8,128)(2,1)} fusion(bf16[1,256,4608]{2,1,0:T(8,128)(2,1)S(1)} %fusion.1, bf16[1,256,4608]{2,1,0:T(8,128)(2,1)S(1)} %fusion.2), kind=kLoop, calls=%fused_computation.16 | loop fusion | flops 2359296 | bytes 9437184 | tf_op jit(solution)/shard_map/stack | solution.py:412
  73.5 37.0 %scatter_sum.1 = f32[2,16,4608]{2,1,0:T(8,128)} custom-call(bf16[2,256,4608]{2,1,0:T(8,128)(2,1)} %pad_maximum_fusion.part_ref), custom_call_target="tpu_custom_call" | custom-call | tf_op jit(solution)/shard_map/scatter_sum/pallas_call | solution.py:361
  110.5 1.9 %fusion.56 = (bf16[2,16,4608]{2,1,0:T(8,128)(2,1)}, f32[16,2,4608]{2,0,1:T(8,128)S(1)}) fusion(f32[2,16,4608]{2,1,0:T(8,128)} %scatter_sum.1, bf16[16,2,4608]{2,1,0:T(2,128)(2,1)S(1)} %copy-done.4, f32[2,4608]{1,0:T(2,128)S(1)} %copy-done.5), kind=kLoop, calls=%fused_computation.65 | loop fusion | flops 737280 | bytes 1806336 | tf_op jit(solution)/shard_map/convert_element_type | solution.py:420
  112.4 1.3 copy.14
  113.7 36.4 %gather_rows_16.1 = bf16[2,256,4608]{2,1,0:T(8,128)(2,1)} custom-call(bf16[2,16,4608]{2,1,0:T(8,128)(2,1)} %get-tuple-element.10.own_ref), custom_call_target="tpu_custom_call" | custom-call | tf_op jit(solution)/shard_map/gather_rows_16/pallas_call | solution.py:204
  150.1 3.9 %convert_reduce_fusion = f32[2,4608]{1,0:T(2,128)} fusion(bf16[2,256,4608]{2,1,0:T(8,128)(2,1)} %gather_rows_16.1), kind=kLoop, calls=%fused_computation | loop fusion | flops 4709376 | bytes 4755456 | tf_op jit(solution)/shard_map/reduce_sum | solution.py:429
  154.0 0.8 fusion.91
  154.8 0.8 fusion.22
  155.6 0.8 fusion.90
  156.4 0.6 pad_maximum_fusion.3
  157.0 0.4 convolution_convert_fusion.6
  157.4 0.5 fusion.7
  158.0 0.8 fusion.4
  158.8 0.8 fusion.3
  159.6 0.2 pad_maximum_fusion.2
  159.9 2.4 %copy.15 = bf16[2,4608,128]{2,1,0:T(8,128)(2,1)} copy(bf16[2,4608,128]{1,2,0:T(8,128)(2,1)S(1)} %pad_maximum_fusion.2) | data formatting | bytes 4718592
  162.3 2.2 %fusion.6 = bf16[1,128,4608]{2,1,0:T(8,128)(2,1)S(1)} fusion(bf16[256,128]{1,0:T(8,128)(2,1)} %copy-done.2, bf16[2,256,4608]{2,1,0:T(8,128)(2,1)} %gather_rows_16.1), kind=kOutput, calls=%fused_computation.14 | convolution fusion | flops 302579712 | bytes 3604480 | tf_op jit(solution)/shard_map/dot_general | solution.py:426
  164.6 2.2 %fusion.5 = bf16[1,128,4608]{2,1,0:T(8,128)(2,1)S(1)} fusion(bf16[256,128]{1,0:T(8,128)(2,1)S(1)} %copy-done.3, bf16[2,256,4608]{2,1,0:T(8,128)(2,1)} %gather_rows_16.1), kind=kOutput, calls=%fused_computation.13 | convolution fusion | flops 302579712 | bytes 3604480 | tf_op jit(solution)/shard_map/dot_general | solution.py:426
  166.7 2.0 %pad_maximum_fusion.1 = bf16[3,128,4608]{2,1,0:T(8,128)(2,1)} fusion(bf16[1,128,4608]{2,1,0:T(8,128)(2,1)S(1)} %fusion.7, bf16[1,128,4608]{2,1,0:T(8,128)(2,1)S(1)} %fusion.6, bf16[1,128,4608]{2,1,0:T(8,128)(2,1)S(1)} %fusion.5), kind=kLoop, calls=%fused_computation.27 | loop fusion | flops 3538944 | bytes 7077888 | tf_op jit(solution)/shard_map/stack | solution.py:428
  (20 shorter events, 0.0 us)
Async XLA Ops:
  3.3 57.0 %copy-start.7 = (bf16[2,4608,128]{2,1,0:T(8,128)(2,1)S(1)}, bf16[2,4608,128]{2,1,0:T(8,128)(2,1)}, u32[]{:S(2)}) copy-start(bf16[2,4608,128]{2,1,0:T(8,128)(2,1)} %param.10) | copy-start | bytes 7077892
  64.1 3.9 %copy-start.6 = (s32[256]{0:T(256)S(1)}, s32[256]{0:T(256)}, u32[]{:S(2)}) copy-start(s32[256]{0:T(256)} %param.8) | copy-start | bytes 3076
  64.1 4.4 %copy-start.1 = (bf16[3,128,4608]{2,1,0:T(8,128)(2,1)S(1)}, bf16[3,128,4608]{2,1,0:T(8,128)(2,1)}, u32[]{:S(2)}) copy-start(bf16[3,128,4608]{2,1,0:T(8,128)(2,1)} %param.12) | copy-start | bytes 10616836
  68.5 0.8 copy-start.2
  73.5 37.0 %copy-start.4 = (bf16[16,2,4608]{2,1,0:T(2,128)(2,1)S(1)}, bf16[16,2,4608]{2,1,0:T(2,128)(2,1)}, u32[]{:S(2)}) copy-start(bf16[16,2,4608]{2,1,0:T(2,128)(2,1)} %param.9) | copy-start | bytes 884740
  73.5 37.0 %copy-start.5 = (f32[2,4608]{1,0:T(2,128)S(1)}, f32[2,4608]{1,0:T(2,128)}, u32[]{:S(2)}) copy-start(f32[2,4608]{1,0:T(2,128)} %param.13) | copy-start | bytes 110596
  150.1 3.9 %copy-start = (bf16[2,256,4608]{2,1,0:T(8,128)(2,1)S(1)}, bf16[2,256,4608]{2,1,0:T(8,128)(2,1)}, u32[]{:S(2)}) copy-start(bf16[2,256,4608]{2,1,0:T(8,128)(2,1)} %gather_rows_16.1) | copy-start | bytes 14155780
  150.1 7.9 %slice-start = ((s8[9437184]{0:T(1024)(128)(4,1)}), s8[4194304]{0:T(1024)(128)(4,1)S(1)}, s32[]{:S(2)}) async-start(s8[9437184]{0:T(1024)(128)(4,1)} %bitcast.104), calls=%async_computation | async-start | bytes 8388608
  154.0 3.9 %slice-start.1 = ((s8[9437184]{0:T(1024)(128)(4,1)}), s8[4194304]{0:T(1024)(128)(4,1)S(1)}, s32[]{:S(2)}) async-start(s8[9437184]{0:T(1024)(128)(4,1)} %bitcast.104), calls=%async_computation.1 | async-start | bytes 8388608
  155.6 2.4 %slice-start.2 = ((s8[9437184]{0:T(1024)(128)(4,1)}), s8[1048576]{0:T(1024)(128)(4,1)S(1)}, s32[]{:S(2)}) async-start(s8[9437184]{0:T(1024)(128)(4,1)} %bitcast.104), calls=%async_computation.2 | async-start | bytes 2097152
  162.3 2.2 %copy-start.3 = (bf16[256,128]{1,0:T(8,128)(2,1)S(1)}, bf16[256,128]{1,0:T(8,128)(2,1)}, u32[]{:S(2)}) copy-start(bf16[256,128]{1,0:T(8,128)(2,1)} %copy-done.2) | copy-start | bytes 196612
